TPU v7x, 128 devices: a whole 4x4x4 slice. The times are simulated.
128 devices in a mesh: grp: 4 (over y), dom: 32 (over x, z, core).
Axes of the slice: x: 4, y: 4, z: 4, core: 2. Of those that a mesh axis runs over, the one named last changes fastest.
Arguments:
- grad_rhs: float32 [4096, 320], P(('grp', 'dom')), may hold values from -41 to 41
- block_inv: bfloat16 [4096, 320, 320], P(('grp', 'dom')), may hold values from -1 to 3
- face_jac: bfloat16 [4096, 6, 80, 80], P(('grp', 'dom')), may hold values from -0.3125 to 0.3125
- face_nbr: int32 [4096, 6], P(('grp', 'dom')), may hold values from -1 to 95, as said below
- recv_node: int32 [65536], P(('grp', 'dom')), may hold values from 0 to 2047
- owners: int32 [65536, 1], P(('grp', 'dom')), may hold values from 0 to 127; in each aligned block of 512 rows (0 to 511, 512 to 1023, ...) at most 8 rows name the same one
- donor_elem: int32 [65536], P(('grp', 'dom')), may hold values from 0 to 31
- donor_coords: float32 [3, 65536], P(None, ('grp', 'dom')), may hold values from -1 to 1
- recv_counts: int32 [128, 4], P(('grp', 'dom')), may hold values from 1 to 128, 416 in all within a row
Outputs:
- adjoint_sol: float32 [4096, 320], P(('grp', 'dom'))
Inputs may be any that keep to these rules, and one draw needn't show every extreme that they name: `face_nbr`: each entry is -1 (outer boundary), an element of the same device (below 32), a low interface slot (32 to 63, facing the device one lower along dom) or a high interface slot; on each device every interface slot is named by exactly one face, local neighbours are mutual through face f xor 1, and low slot k faces high slot k of the lower device. `owners`: no owner is named by more than 8 of one device's 512 rows.
All inputs are finite; a program needn't handle non-finite values.
Results may differ from a plain program's by a relative error of at most 0.0018.
Values sent between devices are 32-bit elements; how exact they have to be, the bound alone decides.
No kernel may reach another device: no remote copies, remote signals or barrier semaphores. Data moves between devices by JAX's collectives and lax.ppermute only.
A program may use at most 64 MiB of HBM per device.

v0:
```python
import jax
import jax.numpy as jnp
import numpy as np
from jax import lax
from jax.sharding import PartitionSpec as P

NODES = 64
ELX = 1
ITERS = 2


gll_nodes = (-1.0, -0.4472135954999579, 0.4472135954999579, 1.0)
small_eps = 1e-06


def extended(cells, sides, width):
    for axis, dim in sides:
        count = lax.axis_size(axis)
        ends = count - 1
        head = lax.slice_in_dim(cells, 0, width, axis=dim)
        tail = lax.slice_in_dim(cells, cells.shape[dim] - width, cells.shape[dim], axis=dim)
        cells = jnp.concatenate(
            [
                lax.ppermute(tail, axis, [(i, (i + 1) % count) for i in range(ends)]),
                cells,
                lax.ppermute(head, axis, [((i + 1) % count, i) for i in range(ends)]),
            ],
            axis=dim,
        )
    return cells


def lagrange(coord):
    factors = []
    for k in range(4):
        factor = jnp.ones_like(coord)
        for m in range(4):
            if m != k:
                factor = factor * ((coord - gll_nodes[m]) / (gll_nodes[k] - gll_nodes[m]))
        factors.append(factor)
    return jnp.stack(factors, axis=-1)


def basis_weights(coords):
    along_x = lagrange(coords[0])
    along_y = lagrange(coords[1])
    along_z = lagrange(coords[2])
    product = along_x[:, :, None, None] * along_y[:, None, :, None] * along_z[:, None, None, :]
    return product.reshape(coords.shape[1], 64)


def face_table():
    node_grid = np.arange(64).reshape(4, 4, 4)
    face_list = [
        node_grid[0],
        node_grid[3],
        node_grid[:, 0],
        node_grid[:, 3],
        node_grid[:, :, 0],
        node_grid[:, :, 3],
    ]
    return np.stack([one_face.reshape(16) for one_face in face_list]).astype(np.int32)


def least_squares(columns, start_norm):
    count_cols = len(columns)
    cosines = []
    sine_vals = []
    rhs_vec = [start_norm] + [start_norm * 0.0 for k in range(count_cols)]
    triangle = []
    for j in range(count_cols):
        column = list(columns[j])
        for i in range(j):
            upper_one = column[i]
            lower_one = column[i + 1]
            column[i] = cosines[i] * upper_one + sine_vals[i] * lower_one
            column[i + 1] = cosines[i] * lower_one - sine_vals[i] * upper_one
        radius = jnp.sqrt(column[j] * column[j] + column[j + 1] * column[j + 1])
        cosine = column[j] / radius
        sine_val = column[j + 1] / radius
        cosines.append(cosine)
        sine_vals.append(sine_val)
        column[j] = radius
        triangle.append(column[: j + 1])
        rhs_vec[j + 1] = -sine_val * rhs_vec[j]
        rhs_vec[j] = cosine * rhs_vec[j]
    coeffs = [None] * count_cols
    for j in reversed(range(count_cols)):
        partial_val = rhs_vec[j]
        for k in range(j + 1, count_cols):
            partial_val = partial_val - triangle[k][j] * coeffs[k]
        coeffs[j] = partial_val / triangle[j][j]
    return coeffs


def to_owners(payload, donor_ids):
    return (
        lax.all_to_all(payload, ("grp", "dom"), split_axis=0, concat_axis=0, tiled=True),
        lax.all_to_all(donor_ids, ("grp", "dom"), split_axis=0, concat_axis=0, tiled=True),
    )


def local(
    grad_rhs,
    block_inv,
    face_jac,
    face_nbr,
    recv_node,
    owners,
    donor_elem,
    donor_coords,
    recv_counts,
):
    elements = block_inv.shape[0]
    block_w = block_inv.shape[1]
    var_count = block_w // NODES
    face_w = face_jac.shape[2]
    face_pts = face_w // var_count
    ifaces = elements // ELX
    points = recv_node.shape[0]
    peers = lax.axis_size("grp") * lax.axis_size("dom")
    capacity = 2 * points // peers
    slots = peers * capacity
    face_nodes = face_table()
    opposite = jnp.array([1, 0, 3, 2, 5, 4], jnp.int32)[None, :]
    source = jnp.where(
        face_nbr < 0,
        elements * 6 + 2 * ifaces,
        jnp.where(face_nbr < elements, face_nbr * 6 + opposite, elements * 6 + face_nbr - elements),
    )
    slot_idx = jnp.where(face_nbr >= elements, face_nbr - elements, 2 * ifaces).reshape(
        elements * 6
    )
    live_mask = (
        (jnp.arange(128, dtype=jnp.int32)[None, :] < recv_counts[0][:, None])
        .reshape(points)
        .astype(jnp.float32)
    )
    source_elem = recv_node // NODES
    source_node = recv_node % NODES
    owner_col = owners[:, 0]
    owner_hot = (owner_col[:, None] == jnp.arange(peers, dtype=jnp.int32)[None, :]).astype(
        jnp.int32
    )
    rank_in_owner = jnp.sum((jnp.cumsum(owner_hot, axis=0) - owner_hot) * owner_hot, axis=1)
    send_slot = owner_col * capacity + rank_in_owner
    ids_out = jnp.zeros((slots,), jnp.int32).at[send_slot].set(donor_elem).reshape(peers, capacity)
    element_row = jnp.arange(elements, dtype=jnp.int32)[:, None]
    recv_weights = basis_weights(donor_coords)
    start_norm = jnp.sqrt(lax.psum(jnp.sum(grad_rhs * grad_rhs), ("grp", "dom")) + small_eps)
    krylov = [grad_rhs / start_norm]
    columns = []
    for j in range(ITERS):
        vector = krylov[j]
        rounded = vector.astype(jnp.bfloat16)
        solved = jnp.einsum(
            "eij,ei->ej", block_inv, rounded, preferred_element_type=jnp.float32
        ).astype(jnp.bfloat16)
        nodal_vals = solved.reshape(elements, var_count, NODES)
        traces = nodal_vals[:, :, face_nodes].transpose(0, 2, 1, 3).reshape(elements, 6, face_w)
        face_out = jnp.einsum("efab,efa->efb", face_jac, traces, preferred_element_type=jnp.float32)
        flat_out = face_out.reshape(elements * 6, face_w)
        outgoing = jnp.zeros((2 * ifaces + 1, face_w), jnp.float32).at[slot_idx].add(flat_out)
        outgoing = outgoing[: 2 * ifaces].reshape(2, ifaces, face_w)
        padded = extended(outgoing, (("dom", 0),), 1)
        trace_pool = jnp.concatenate(
            [flat_out, padded[0], padded[3], jnp.zeros((1, face_w), jnp.float32)]
        )
        incoming = (
            trace_pool[source].reshape(elements, 6, var_count, face_pts).transpose(0, 2, 1, 3)
        )
        face_sum = (
            jnp.zeros((elements, var_count, NODES), jnp.float32).at[:, :, face_nodes].add(incoming)
        )
        picked = nodal_vals[source_elem, :, source_node].astype(jnp.float32) * live_mask[:, None]
        contrib = (picked[:, :, None] * recv_weights[:, None, :]).reshape(points, block_w)
        values_out = jnp.zeros((slots, block_w), jnp.float32).at[send_slot].set(contrib)
        got_vals, got_ids = to_owners(values_out.reshape(peers, capacity, block_w), ids_out)
        got_contrib = got_vals.reshape(slots, block_w)
        id_hot = (element_row == got_ids.reshape(1, slots)).astype(jnp.float32)
        interp_sum = jnp.dot(id_hot, got_contrib, precision=lax.Precision.HIGHEST)
        mapped = vector - face_sum.reshape(elements, block_w) - interp_sum
        heights = []
        for i in range(j + 1):
            height = lax.psum(jnp.sum(mapped * krylov[i]), ("grp", "dom"))
            mapped = mapped - height * krylov[i]
            heights.append(height)
        length = jnp.sqrt(lax.psum(jnp.sum(mapped * mapped), ("grp", "dom")) + small_eps)
        krylov.append(mapped / length)
        columns.append(heights + [length])
    coeffs = least_squares(columns, start_norm)
    result = coeffs[0] * krylov[0]
    j = 1
    result = result + coeffs[j] * krylov[j]
    return result


def solution(mesh):
    placed = (
        P(("grp", "dom"), None),
        P(("grp", "dom"), None, None),
        P(("grp", "dom"), None, None, None),
        P(("grp", "dom"), None),
        P(("grp", "dom")),
        P(("grp", "dom"), None),
        P(("grp", "dom")),
        P(None, ("grp", "dom")),
        P(("grp", "dom"), None),
    )
    return jax.shard_map(
        local, mesh=mesh, in_specs=placed, out_specs=P(("grp", "dom"), None), check_vma=False
    )
```

profile of v0, /device:TPU:1, one launch (start us, length us, event | category | flops | bytes accessed | tf_op | source)
XLA Modules:
  0.0 504.7 jit_solution(4689011227324642660)
XLA Ops:
  0.0 0.9 copy.83
  0.9 0.2 fusion.16
  1.2 0.9 fusion.15
  2.1 2.6 scatter_custom_fusion.2
  4.7 0.7 all_to_all.13
  5.4 11.5 %all-to-all-start = ((s32[128,1,8]{2,1,0:T(1,128)}), s32[128,1,8]{2,1,0:T(1,128)S(1)}, u32[]{:S(2)}, u32[]{:S(2)}) async-start(s32[128,1,8]{2,1,0:T(1,128)} %bitcast.22), calls=%async_computation | async-start | bytes 131072 | tf_op jit(solution)/shard_map/all_to_all | solution.py:99
  17.0 0.6 multiply_reduce_fusion.5
  17.8 67.2 %psum.42 = f32[]{:T(128)} all-reduce(f32[]{:T(128)} %multiply_reduce_fusion.5), channel_id=1, replica_groups=mesh['grp'=4,'dom'=32] {'grp','dom'}, use_global_device_ids=true, to_apply=%region_1.2 | all-reduce | flops 1 | bytes 8 | tf_op jit(solution)/shard_map/psum | solution.py:150
  85.7 4.4 fusion.23
  90.3 0.4 copy.86
  90.7 3.2 gather_fusion.2
  93.9 0.1 copy.87
  94.2 0.1 copy.76
  94.3 0.3 copy.88
  94.6 0.7 gather_fusion
  95.3 0.1 copy.99
  95.4 3.5 scatter_custom_fusion.3
  98.9 4.7 all-to-all-start.1
  103.6 3.2 fusion.38
  107.2 1.5 scatter_custom_fusion
  108.7 3.0 collective-permute-start.1
  111.7 2.8 collective-permute-start
  114.7 0.5 broadcast.940
  115.2 0.8 reduce.3
  116.1 2.7 collective-permute-done.1
  118.9 0.7 gather_fusion.1
  119.6 0.2 reshape.685
  119.8 0.4 copy.105
  120.2 3.8 scatter_fusion
  124.0 0.2 copy.82
  124.3 4.0 all-to-all-done.1
  128.3 1.3 multiply_reduce_fusion.4
  129.6 66.0 %psum.43 = f32[]{:T(128)} all-reduce(f32[]{:T(128)} %get-tuple-element.25), channel_id=1, replica_groups=mesh['grp'=4,'dom'=32] {'grp','dom'}, use_global_device_ids=true, to_apply=%region_10.11 | all-reduce | flops 1 | bytes 8 | tf_op jit(solution)/shard_map/psum | solution.py:185
  195.6 1.3 multiply_reduce_fusion.3
  197.0 62.6 %psum.44 = f32[]{:T(128)} all-reduce(f32[]{:T(128)} %multiply_reduce_fusion.3), channel_id=1, replica_groups=mesh['grp'=4,'dom'=32] {'grp','dom'}, use_global_device_ids=true, to_apply=%region_12.13 | all-reduce | flops 1 | bytes 8 | tf_op jit(solution)/shard_map/psum | solution.py:188
  260.3 0.7 convert_bitcast_fusion
  260.9 4.4 fusion.21
  265.5 0.4 copy.94
  265.9 3.2 gather_fusion.5
  269.1 0.1 copy.95
  269.3 0.3 copy.96
  269.5 3.5 scatter_custom_fusion.6
  273.0 5.3 %all-to-all-start.2 = ((f32[128,8,320]{2,1,0:T(8,128)}), f32[128,8,320]{2,1,0:T(8,128)S(1)}, u32[]{:S(2)}, u32[]{:S(2)}) async-start(f32[128,8,320]{2,1,0:T(8,128)} %bitcast.55), calls=%async_computation.2 | async-start | bytes 3145728 | tf_op jit(solution)/shard_map/all_to_all | solution.py:98
  278.3 0.1 copy.89
  278.4 0.7 gather_fusion.3
  279.1 0.1 copy.103
  279.2 3.2 fusion.39
  282.5 1.5 scatter_custom_fusion.4
  284.0 3.7 collective-permute-start.2
  287.7 2.1 collective-permute-start.3
  291.9 1.5 collective-permute-done.3
  293.5 0.7 gather_fusion.4
  294.2 0.2 reshape.693
  294.4 0.4 copy.106
  294.8 3.8 scatter_fusion.1
  298.7 0.2 copy.93
  298.9 4.0 all-to-all-done.2
  302.9 1.3 multiply_reduce_fusion.2
  304.2 66.5 %psum.45 = f32[]{:T(128)} all-reduce(f32[]{:T(128)} %get-tuple-element.27), channel_id=1, replica_groups=mesh['grp'=4,'dom'=32] {'grp','dom'}, use_global_device_ids=true, to_apply=%region_17.18 | all-reduce | flops 1 | bytes 8 | tf_op jit(solution)/shard_map/psum | solution.py:185
  370.7 1.3 multiply_reduce_fusion.1
  372.6 62.8 %psum.46 = f32[]{:T(128)} all-reduce(f32[]{:T(128)} %multiply_reduce_fusion.1), channel_id=1, replica_groups=mesh['grp'=4,'dom'=32] {'grp','dom'}, use_global_device_ids=true, to_apply=%region_19.20 | all-reduce | flops 1 | bytes 8 | tf_op jit(solution)/shard_map/psum | solution.py:185
  435.9 1.9 multiply_reduce_fusion
  439.1 64.1 %psum.47 = f32[]{:T(128)} all-reduce(f32[]{:T(128)} %multiply_reduce_fusion), channel_id=1, replica_groups=mesh['grp'=4,'dom'=32] {'grp','dom'}, use_global_device_ids=true, to_apply=%region_21.22 | all-reduce | flops 1 | bytes 8 | tf_op jit(solution)/shard_map/psum | solution.py:188
  504.1 0.6 multiply_add_fusion
  (67 shorter events, 1.9 us)
Async XLA Ops:
  0.0 2.1 copy-start.2
  0.0 16.9 %copy-start.3 = (f32[3,512]{1,0:T(4,128)S(1)}, f32[3,512]{1,0:T(4,128)}, u32[]{:S(2)}) copy-start(f32[3,512]{1,0:T(4,128)} %param.22) | copy-start | bytes 18436
  0.0 17.0 %copy-start = (f32[32,320]{1,0:T(8,128)S(1)}, f32[32,320]{1,0:T(8,128)}, u32[]{:S(2)}) copy-start(f32[32,320]{1,0:T(8,128)} %param.15) | copy-start | bytes 122884
  5.4 93.5 %all-to-all-start = ((s32[128,1,8]{2,1,0:T(1,128)}), s32[128,1,8]{2,1,0:T(1,128)S(1)}, u32[]{:S(2)}, u32[]{:S(2)}) async-start(s32[128,1,8]{2,1,0:T(1,128)} %bitcast.22), calls=%async_computation | async-start | bytes 131072 | tf_op jit(solution)/shard_map/all_to_all | solution.py:99
  85.7 4.9 copy-start.5
  90.2 3.8 copy-start.6
  90.2 4.0 copy-start.1
  98.9 29.4 %all-to-all-start.1 = ((f32[128,8,320]{2,1,0:T(8,128)}), f32[128,8,320]{2,1,0:T(8,128)S(1)}, u32[]{:S(2)}, u32[]{:S(2)}) async-start(f32[128,8,320]{2,1,0:T(8,128)} %bitcast.38), calls=%async_computation.1 | async-start | bytes 3145728 | tf_op jit(solution)/shard_map/all_to_all | solution.py:98
  103.6 3.3 copy-start.4
  103.6 3.3 copy-start.7
  108.7 10.1 %collective-permute-start.1 = (f32[1,32,80]{2,1,0:T(8,128)S(1)}, f32[1,32,80]{2,1,0:T(8,128)S(1)}, u32[]{:S(2)}, u32[]{:S(2)}) collective-permute-start(f32[1,32,80]{2,1,0:T(8,128)S(1)} %get-tuple-element.10), channel_id=1, source_target_pairs={{1,0},{2,1},{3,2},{4,3},{5,4},{6,5},{7,6},{8,7},{9,8},{10,9},{11,1... | collective-permute-start | bytes 30728 | tf_op jit(solution)/shard_map/ppermute | solution.py:26
  111.7 7.1 %collective-permute-start = (f32[1,32,80]{2,1,0:T(8,128)S(1)}, f32[1,32,80]{2,1,0:T(8,128)S(1)}, u32[]{:S(2)}, u32[]{:S(2)}) collective-permute-start(f32[1,32,80]{2,1,0:T(8,128)S(1)} %get-tuple-element.9), channel_id=1, source_target_pairs={{0,1},{1,2},{2,3},{3,4},{4,5},{5,6},{6,7},{7,8},{8,9},{9,10},{10,1... | collective-permute-start | bytes 30728 | tf_op jit(solution)/shard_map/ppermute | solution.py:24
  273.0 30.0 %all-to-all-start.2 = ((f32[128,8,320]{2,1,0:T(8,128)}), f32[128,8,320]{2,1,0:T(8,128)S(1)}, u32[]{:S(2)}, u32[]{:S(2)}) async-start(f32[128,8,320]{2,1,0:T(8,128)} %bitcast.55), calls=%async_computation.2 | async-start | bytes 3145728 | tf_op jit(solution)/shard_map/all_to_all | solution.py:98
  284.0 7.9 %collective-permute-start.2 = (f32[1,32,80]{2,1,0:T(8,128)S(1)}, f32[1,32,80]{2,1,0:T(8,128)S(1)}, u32[]{:S(2)}, u32[]{:S(2)}) collective-permute-start(f32[1,32,80]{2,1,0:T(8,128)S(1)} %get-tuple-element.7), channel_id=1, source_target_pairs={{0,1},{1,2},{2,3},{3,4},{4,5},{5,6},{6,7},{7,8},{8,9},{9,10},{10,1... | collective-permute-start | bytes 30728 | tf_op jit(solution)/shard_map/ppermute | solution.py:24
  287.7 5.7 %collective-permute-start.3 = (f32[1,32,80]{2,1,0:T(8,128)S(1)}, f32[1,32,80]{2,1,0:T(8,128)S(1)}, u32[]{:S(2)}, u32[]{:S(2)}) collective-permute-start(f32[1,32,80]{2,1,0:T(8,128)S(1)} %get-tuple-element.8), channel_id=1, source_target_pairs={{1,0},{2,1},{3,2},{4,3},{5,4},{6,5},{7,6},{8,7},{9,8},{10,9},{11,1... | collective-permute-start | bytes 30728 | tf_op jit(solution)/shard_map/ppermute | solution.py:26
where the time goes:
time: 506 us; the launch traced here: 505 us
  blocking collectives  389 us (77%)
  starting transfers between devices  33 us (7%)
  local copies, waits for them, and re-layouts  25.3 us (5%)
  other arithmetic  19.6 us (4%)
  matrix products  17.9 us (4%)
  waiting for transfers between devices  12.3 us (2%)
  between operations  7.36 us (1%)
    psum x3, blocking collectives, local(): height = lax.psum(jnp.sum(mapped * krylov[i]), ('grp', 'dom'))  195 us
    psum x2, blocking collectives, local(): lax.psum(jnp.sum(mapped * mapped), ('grp', 'dom')) + small_eps  127 us
    psum x1, blocking collectives, local(): lax.psum(jnp.sum(grad_rhs * grad_rhs), ('grp', 'dom')) + small_eps  67.2 us
    all_to_all x1, starting transfers between devices, to_owners(): lax.all_to_all(donor_ids, ('grp', 'dom'), split_axis=0, concat_axis=0, ti...  11.5 us
  transfers between devices with their start and end apart: 7, of which 4 were waited for; matrix products, arithmetic and copies ran while one was open for 7% of the time, Pallas kernels for 0%

commit v1 on v0

v1 whole, which is shorter than its diff:
```python
import jax
import jax.numpy as jnp
import numpy as np
from jax import lax
from jax.experimental import pallas as pl
from jax.experimental.pallas import tpu as pltpu
from jax.sharding import PartitionSpec as P

AXES = ("grp", "dom")
VARS = 5
NODES = 64
BLOCK = 320
FACEW = 80
E = 32
PEERS = 128
CAP = 8
RPTS = 512
CHUNKS = 8
SCALAR_LANE = 96
GLL = (-1.0, -0.4472135954999579, 0.4472135954999579, 1.0)
EPS = 1e-06
F32 = jnp.float32
BF16 = jnp.bfloat16
VMEM_LIMIT = 40 * 1024 * 1024


def face_table():
    grid = np.arange(64).reshape(4, 4, 4)
    faces = [grid[0], grid[3], grid[:, 0], grid[:, 3], grid[:, :, 0], grid[:, :, 3]]
    return np.stack([one.reshape(16) for one in faces])


def spread_matrix():
    table = face_table()
    out = np.zeros((6, VARS, 16, BLOCK), np.float32)
    for f in range(6):
        for v in range(VARS):
            out[f, v, np.arange(16), v * NODES + table[f]] = 1.0
    return out.reshape(6 * FACEW, BLOCK)


def dot(a, b):
    return jnp.dot(a, b, preferred_element_type=F32)


def dot_nt(a, b):
    return lax.dot_general(a, b, (((1,), (1,)), ((), ())), preferred_element_type=F32)


def dot_tn(a, b):
    return lax.dot_general(a, b, (((0,), (0,)), ((), ())), preferred_element_type=F32)


def split(x):
    hi = x.astype(BF16).astype(F32)
    return hi, x - hi


def iota(shape, dim):
    return lax.broadcasted_iota(jnp.int32, shape, dim)


def total(x):
    return jnp.sum(jnp.sum(x, axis=0, keepdims=True), axis=1, keepdims=True)


def stream(src, dst, sems):
    step = src.shape[0] // CHUNKS
    return [
        pltpu.make_async_copy(
            src.at[pl.ds(c * step, step)], dst.at[pl.ds(c * step, step)], sems.at[c]
        )
        for c in range(CHUNKS)
    ]


def block_solve(x, blocks, copies):
    step = E // CHUNKS
    row = iota((16, BLOCK), 0) % 8
    parts = []
    for g in range(E // 8):
        hi, lo = split(x[8 * g : 8 * g + 8])
        both = jnp.concatenate([hi, lo], axis=0)
        acc = None
        for k in range(8):
            e = 8 * g + k
            if e % step == 0:
                copies[e // step].wait()
            one = dot(jnp.where(row == k, both, 0.0).astype(BF16), blocks[e])
            acc = one if acc is None else acc + one
        parts.append(acc[:8] + acc[8:])
    return jnp.concatenate(parts, axis=0)


def pick(z, recv_node, counts):
    hi, lo = split(z)
    rows = [part[:, v * NODES : (v + 1) * NODES] for part in (hi, lo) for v in range(VARS)]
    rows = jnp.concatenate(rows, axis=0).astype(BF16)
    elem = lax.shift_right_logical(recv_node, 6)
    node = jnp.bitwise_and(recv_node, NODES - 1)
    node_hot = (iota((NODES, RPTS), 0) == node).astype(F32).astype(BF16)
    at_node = dot(rows, node_hot)
    at_node = at_node[: VARS * E] + at_node[VARS * E :]
    lane = iota((1, RPTS), 1)
    block = lax.shift_right_logical(lane, 7)
    count = jnp.where(
        block == 0, counts[0], jnp.where(block == 1, counts[1], jnp.where(block == 2, counts[2], counts[3]))
    )
    live = jnp.bitwise_and(lane, 127) < count
    elem = jnp.where(live, elem, -1)
    elem_hot = iota((E, RPTS), 0) == elem
    return [
        jnp.sum(jnp.where(elem_hot, at_node[v * E : (v + 1) * E], 0.0), axis=0, keepdims=True)
        for v in range(VARS)
    ]


def pack(owner_hot, rank, comps):
    slot = iota((CAP, RPTS), 0) == rank
    rows = [jnp.where(slot, comp, 0.0) for comp in comps]
    rows.append(jnp.zeros((PEERS - CAP * len(comps), RPTS), F32))
    rows = jnp.concatenate(rows, axis=0)
    hi, rest = split(rows)
    mid, low = split(rest)
    out = dot_nt(owner_hot, jnp.concatenate([hi, mid, low], axis=0).astype(BF16))
    return (out[:, :PEERS] + out[:, PEERS : 2 * PEERS]) + out[:, 2 * PEERS :]


def owner_one_hot(owners):
    return (iota((PEERS, RPTS), 0) == owners).astype(F32)


def lagrange(coord):
    factors = []
    for k in range(4):
        factor = None
        for m in range(4):
            if m != k:
                one = (coord - GLL[m]) * (1.0 / (GLL[k] - GLL[m]))
                factor = one if factor is None else factor * one
        factors.append(factor)
    return factors


def interpolate(values, geometry, table):
    values = values.T
    geometry = geometry.T
    val = [values[8 * c : 8 * c + 8] for c in range(VARS)]
    parts = [split(one) for one in val]
    coords = [geometry[8 * (VARS + c) : 8 * (VARS + c) + 8] for c in range(3)]
    rows = [one for coord in coords for one in lagrange(coord)]
    rows.append(geometry[8 * (VARS + 3) : 8 * (VARS + 3) + 8])
    rows += [part[0] for part in parts] + [part[1] for part in parts]
    for c, one in enumerate(rows):
        table[8 * c : 8 * c + 8, :] = one
    sub = iota((8, PEERS), 0)
    elem_id = iota((E, PEERS), 0).astype(F32)
    left = []
    right = []
    for k in range(CAP):

        def row(c):
            return table[pl.ds(8 * c + k, 1), :]

        inner = sub % 4
        along_z = jnp.where(
            inner == 0, row(8), jnp.where(inner == 1, row(9), jnp.where(inner == 2, row(10), row(11)))
        )
        lower = jnp.where(sub < 4, row(4), row(5)) * along_z
        upper = jnp.where(sub < 4, row(6), row(7)) * along_z
        basis = jnp.concatenate(
            [half * row(i) for i in range(4) for half in (lower, upper)], axis=0
        )
        hi, lo = split(basis)
        right.append(jnp.concatenate([hi, lo], axis=0).astype(BF16))
        mask = elem_id == row(12)
        left.append(
            jnp.concatenate(
                [jnp.where(mask, row(13 + c), 0.0) for c in range(2 * VARS)], axis=0
            ).astype(BF16)
        )
    out = dot_nt(jnp.concatenate(left, axis=1), jnp.concatenate(right, axis=1))
    half = VARS * E
    out = out[:half, :NODES] + (out[:half, NODES:] + out[half:, :NODES])
    return jnp.concatenate([out[v * E : (v + 1) * E] for v in range(VARS)], axis=1)


def first_kernel(
    x_ref, blocks_ref, node_ref, owner_ref, elem_ref, coord_ref, count_ref,
    z_ref, pay_ref, rank_ref, buf, sems,
):
    copies = stream(blocks_ref, buf, sems)
    for one in copies:
        one.start()
    hot = owner_one_hot(owner_ref[...])
    hot16 = hot.astype(BF16)
    earlier = (iota((RPTS, RPTS), 0) < iota((RPTS, RPTS), 1)).astype(F32).astype(BF16)
    rank = jnp.sum(hot * dot(hot16, earlier), axis=0, keepdims=True).astype(jnp.int32)
    rank_ref[...] = rank
    z = block_solve(x_ref[...], buf, copies)
    z_ref[...] = z
    counts = [count_ref[0, i] for i in range(4)]
    comps = pick(z, node_ref[...], counts)
    comps += [coord_ref[c : c + 1, :] for c in range(3)]
    comps.append(elem_ref[...].astype(F32))
    pay_ref[...] = pack(hot16, rank, comps)


def face_kernel(
    z_ref, x_ref, jac_ref, nbr_ref, spread_ref,
    base_ref, low_ref, high_ref, traces, outs, buf, sems,
):
    copies = stream(jac_ref, buf, sems)
    for one in copies:
        one.start()
    hi, lo = split(z_ref[...])
    traces[...] = dot_nt(jnp.concatenate([hi, lo], axis=0).astype(BF16), spread_ref[...])
    own_face = iota((16, 6 * FACEW), 1) // FACEW == iota((16, 6 * FACEW), 0) % 8
    step = E // CHUNKS
    for e in range(E):
        if e % step == 0:
            copies[e // step].wait()
        both = jnp.concatenate(
            [
                jnp.broadcast_to(traces[pl.ds(e, 1), :], (8, 6 * FACEW)),
                jnp.broadcast_to(traces[pl.ds(E + e, 1), :], (8, 6 * FACEW)),
            ],
            axis=0,
        )
        one = dot(jnp.where(own_face, both, 0.0).astype(BF16), buf[e])
        outs[8 * e : 8 * e + 8, 0:FACEW] = one[:8] + one[8:]
    out = jnp.concatenate(
        [outs[pl.ds(f, E, stride=8), :][:, :FACEW] for f in range(6)], axis=0
    )
    hi, lo = split(out)
    hi, lo = hi.astype(BF16), lo.astype(BF16)
    local_hot, iface_hot = neighbour_one_hots(nbr_ref[...])
    outgoing = dot(iface_hot, hi) + dot(iface_hot, lo)
    low_ref[...] = outgoing[:E]
    high_ref[...] = outgoing[E:]
    incoming = dot_tn(local_hot, hi) + dot_tn(local_hot, lo)
    base_ref[...] = x_ref[...] - spread_faces(incoming, spread_ref)


def neighbour_one_hots(nbr):
    target = jnp.concatenate(
        [
            jnp.where(nbr[f : f + 1] < 0, -1, jnp.where(nbr[f : f + 1] < E, nbr[f : f + 1] + (f ^ 1) * E, nbr[f : f + 1] + 5 * E))
            for f in range(6)
        ],
        axis=1,
    )
    hot = (iota((8 * E, 6 * E), 0) == target).astype(F32).astype(BF16)
    return hot[: 6 * E], hot[6 * E :]


def spread_faces(incoming, spread_ref):
    hi, lo = split(incoming)
    acc = None
    for f in range(6):
        both = jnp.concatenate([hi[f * E : (f + 1) * E], lo[f * E : (f + 1) * E]], axis=0)
        one = dot(both.astype(BF16), spread_ref[f * FACEW : (f + 1) * FACEW, :])
        acc = one if acc is None else acc + one
    return acc[:E] + acc[E:]


def arrived_kernel(base_ref, low_ref, high_ref, nbr_ref, spread_ref, out_ref):
    hi, lo = split(jnp.concatenate([low_ref[...], high_ref[...]], axis=0))
    _, iface_hot = neighbour_one_hots(nbr_ref[...])
    incoming = dot_tn(iface_hot, hi.astype(BF16)) + dot_tn(iface_hot, lo.astype(BF16))
    out_ref[...] = base_ref[...] - spread_faces(incoming, spread_ref)


def with_scalars(table, scalars):
    lane = iota(table.shape, 1)
    for i, one in enumerate(scalars):
        table = jnp.where(lane == SCALAR_LANE + i, one, table)
    return table


def read_scalars(table, count):
    row = jnp.sum(table, axis=0, keepdims=True)
    return [row[:, SCALAR_LANE + i : SCALAR_LANE + i + 1] for i in range(count)]


def second_kernel(
    base_ref, got_ref, b_ref, blocks_ref, node_ref, owner_ref, rank_ref, count_ref,
    u_ref, z_ref, pay_ref, table, buf, sems,
):
    copies = stream(blocks_ref, buf, sems)
    for one in copies:
        one.start()
    got = got_ref[...]
    u = base_ref[...] - interpolate(got, got, table)
    u_ref[...] = u
    b = b_ref[...]
    z = block_solve(u, buf, copies)
    z_ref[...] = z
    counts = [count_ref[0, i] for i in range(4)]
    comps = pick(z, node_ref[...], counts)
    hot = owner_one_hot(owner_ref[...]).astype(BF16)
    pay = pack(hot, rank_ref[...], comps)
    pay_ref[...] = with_scalars(pay, [total(b * b), total(b * u)])


def third_kernel(base_ref, got_ref, first_ref, b_ref, u_ref, rest_ref, pay_ref, known_ref, table):
    got = got_ref[...]
    w = base_ref[...] - interpolate(got, first_ref[...], table)
    bb, bu = read_scalars(got, 2)
    h00 = bu / (bb + EPS)
    b = b_ref[...]
    u = u_ref[...]
    rest = u - h00 * b
    mapped = w - h00 * u
    rest_ref[...] = rest
    scalars = [
        total(rest * rest), total(b * rest), total(mapped * b), total(mapped * rest), total(mapped * mapped),
    ]
    pay_ref[...] = with_scalars(jnp.zeros((PEERS, PEERS), F32), scalars)
    known_ref[...] = with_scalars(jnp.zeros((8, PEERS), F32), [bb * 0.125, bu * 0.125])


def last_kernel(got_ref, known_ref, b_ref, rest_ref, out_ref):
    bb, bu = read_scalars(known_ref[...], 2)
    rr, br, mb, mr, mm = read_scalars(got_ref[...], 5)
    s2 = bb + EPS
    start = jnp.sqrt(s2)
    h00 = bu / s2
    h10 = jnp.sqrt(rr / s2 + EPS)
    h01 = mb / (s2 * h10)
    scale = s2 * (h10 * h10)
    h11 = mr / scale
    left = (
        mm / scale
        - h01 * h01 * (2.0 - bb / s2)
        - h11 * h11 * (2.0 - rr / scale)
        + 2.0 * h01 * h11 * (br / (s2 * h10))
    )
    h21 = jnp.sqrt(jnp.maximum(left, 0.0) + EPS)
    r00 = jnp.sqrt(h00 * h00 + h10 * h10)
    c0 = h00 / r00
    s0 = h10 / r00
    r01 = c0 * h01 + s0 * h11
    low = c0 * h11 - s0 * h01
    r11 = jnp.sqrt(low * low + h21 * h21)
    c1 = low / r11
    y1 = c1 * (-s0 * start) / r11
    y0 = (c0 * start - r01 * y1) / r00
    out_ref[...] = (y0 / start) * b_ref[...] + (y1 / (start * h10)) * rest_ref[...]


VM = pl.BlockSpec(memory_space=pltpu.VMEM)
SM = pl.BlockSpec(memory_space=pltpu.SMEM)
ANY = pl.BlockSpec(memory_space=pl.ANY)


def call(kernel, in_specs, outs, scratch, *args):
    return pl.pallas_call(
        kernel,
        in_specs=in_specs,
        out_specs=[VM] * len(outs),
        out_shape=[jax.ShapeDtypeStruct(shape, dtype) for shape, dtype in outs],
        scratch_shapes=scratch,
        compiler_params=pltpu.CompilerParams(vmem_limit_bytes=VMEM_LIMIT),
        name=kernel.__name__,
    )(*args)


def exchange(table):
    return lax.all_to_all(
        table.reshape(PEERS, 1, PEERS), AXES, split_axis=0, concat_axis=0, tiled=True
    ).reshape(PEERS, PEERS)


def local(
    grad_rhs, block_inv, face_jac, face_nbr, recv_node, owners, donor_elem, donor_coords, recv_counts
):
    jac = face_jac.reshape(E, 6 * FACEW, FACEW)
    nbr = face_nbr.T
    node = recv_node.reshape(1, RPTS)
    owner = owners.reshape(1, RPTS)
    elem = donor_elem.reshape(1, RPTS)
    spread = jnp.asarray(spread_matrix(), BF16)
    ends = lax.axis_size("dom") - 1
    upward = [(i, i + 1) for i in range(ends)]
    downward = [(i + 1, i) for i in range(ends)]
    full = ((E, BLOCK), F32)
    table = ((PEERS, PEERS), F32)
    half = ((E, FACEW), F32)
    block_scratch = [pltpu.VMEM((E, BLOCK, BLOCK), BF16), pltpu.SemaphoreType.DMA((CHUNKS,))]
    rows_scratch = pltpu.VMEM((8 * (13 + 2 * VARS), PEERS), F32)

    def faces(z, x):
        base, low, high = call(
            face_kernel,
            [VM, VM, ANY, VM, VM],
            [full, half, half],
            [
                pltpu.VMEM((2 * E, 6 * FACEW), F32),
                pltpu.VMEM((8 * E, PEERS), F32),
                pltpu.VMEM((E, 6 * FACEW, FACEW), BF16),
                pltpu.SemaphoreType.DMA((CHUNKS,)),
            ],
            z, x, jac, nbr, spread,
        )
        from_lower = lax.ppermute(high, "dom", upward)
        from_upper = lax.ppermute(low, "dom", downward)
        return call(
            arrived_kernel, [VM] * 5, [full], [], base, from_lower, from_upper, nbr, spread
        )[0]

    z1, pay1, rank = call(
        first_kernel,
        [VM, ANY, VM, VM, VM, VM, SM],
        [full, table, ((1, RPTS), jnp.int32)],
        block_scratch,
        grad_rhs, block_inv, node, owner, elem, donor_coords, recv_counts,
    )
    got1 = exchange(pay1)
    base1 = faces(z1, grad_rhs)
    u, z2, pay2 = call(
        second_kernel,
        [VM, VM, VM, ANY, VM, VM, VM, SM],
        [full, full, table],
        [rows_scratch] + block_scratch,
        base1, got1, grad_rhs, block_inv, node, owner, rank, recv_counts,
    )
    got2 = exchange(pay2)
    base2 = faces(z2, u)
    rest, pay3, known = call(
        third_kernel,
        [VM] * 5,
        [full, table, ((8, PEERS), F32)],
        [rows_scratch],
        base2, got2, got1, grad_rhs, u,
    )
    got3 = exchange(pay3)
    return call(last_kernel, [VM] * 4, [full], [], got3, known, grad_rhs, rest)[0]


def solution(mesh):
    placed = (
        P(AXES, None),
        P(AXES, None, None),
        P(AXES, None, None, None),
        P(AXES, None),
        P(AXES),
        P(AXES, None),
        P(AXES),
        P(None, AXES),
        P(AXES, None),
    )
    return jax.shard_map(
        local, mesh=mesh, in_specs=placed, out_specs=P(AXES, None), check_vma=False
    )
```

time: 506 us -> 101 us (0.20)
  blocking collectives: 389 us -> 19.4 us
  Pallas kernels: 0 us -> 27.2 us
  other arithmetic: 19.6 us -> 0 us
  matrix products: 17.9 us -> 0 us
  local copies, waits for them, and re-layouts: 25.3 us -> 14.9 us
  between operations: 7.36 us -> 0.22 us
  waiting for transfers between devices: 12.3 us -> 6.25 us
    psum x6 -> x0, blocking collectives: 389 us -> none  [the longest x3 195 us: local(): height = lax.psum(jnp.sum(mapped * krylov[i]), ('grp', 'dom'))]
    pallas_call x0 -> x8, Pallas kernels: none -> 27.2 us  [call(): pl.pallas_call(kernel, in_specs=in_specs, out_specs=[VM] * len(outs), out...]
    all_to_all x0 -> x1, blocking collectives: none -> 19.4 us  [exchange(): lax.all_to_all(table.reshape(PEERS, 1, PEERS), AXES, split_axis=0, concat...]
    dot_general x6 -> x0, matrix products: 17.9 us -> none  [the longest x2 8.86 us: local(): jnp.einsum('eij,ei->ej', block_inv, rounded, preferred_element_type=jnp.f...]
    unnamed x17 -> x32, local copies, waits for them, and re-layouts: 0.04 us -> 14.9 us
    scatter-add x4 -> x0, other arithmetic: 10.5 us -> none  [the longest x2 7.63 us: local(): jnp.zeros((elements, var_count, NODES), jnp.float32).at[:, :, face_nodes]]
    scatter x3 -> x0, local copies, waits for them, and re-layouts: 9.51 us -> none  [the longest x2 6.9 us: local(): jnp.zeros((slots, block_w), jnp.float32).at[send_slot].set(contrib)]
    gather x10 -> x0, local copies, waits for them, and re-layouts: 9.33 us -> none  [the longest x4 6.57 us: local(): nodal_vals[source_elem, :, source_node].astype(jnp.float32)]
  transfers between devices with their start and end apart: 7 -> 6, of which waited for: 4 -> 2; matrix products, arithmetic and copies ran while one was open for 7% -> 0% of each run, Pallas kernels for 0% -> 11%
where the time goes in v1:
time: 101 us
  starting transfers between devices  32.9 us (33%)
  Pallas kernels  27.2 us (27%)
  blocking collectives  19.4 us (19%)
  local copies, waits for them, and re-layouts  14.9 us (15%)
  waiting for transfers between devices  6.25 us (6%)
    pallas_call x8, Pallas kernels, call(): pl.pallas_call(kernel, in_specs=in_specs, out_specs=[VM] * len(outs), out...  27.2 us
    all_to_all x2, starting transfers between devices, exchange(): lax.all_to_all(table.reshape(PEERS, 1, PEERS), AXES, split_axis=0, concat...  21.7 us
    all_to_all x1, blocking collectives, exchange(): lax.all_to_all(table.reshape(PEERS, 1, PEERS), AXES, split_axis=0, concat...  19.4 us
    unnamed x32, local copies, waits for them, and re-layouts  14.9 us
    ppermute x2, starting transfers between devices, faces(): from_lower = lax.ppermute(high, 'dom', upward)  7.32 us
    ppermute x2, waiting for transfers between devices, faces(): from_upper = lax.ppermute(low, 'dom', downward)  6.24 us
    ppermute x2, starting transfers between devices, faces(): from_upper = lax.ppermute(low, 'dom', downward)  3.84 us
  transfers between devices with their start and end apart: 6, of which 2 were waited for; matrix products, arithmetic and copies ran while one was open for 0% of the time, Pallas kernels for 11%

profile of v1, /device:TPU:1, one launch (start us, length us, event | category | flops | bytes accessed | tf_op | source)
XLA Modules:
  0.0 100.8 jit_solution(584679182810496877)
XLA Ops:
  0.0 0.0 copy-start.15
  0.0 0.0 copy-start.7
  0.0 0.0 copy-start
  0.0 3.3 %copy-done = bf16[32,320,320]{2,1,0:T(8,128)(2,1)S(1)} copy-done((bf16[32,320,320]{2,1,0:T(8,128)(2,1)S(1)}, bf16[32,320,320]{2,1,0:T(8,128)(2,1)}, u32[]{:S(2)}) %copy-start) | copy-done | bytes 6553624
  3.3 0.0 copy-start.5
  3.3 0.8 copy-done.5
  4.1 0.0 copy-start.8
  4.1 0.7 copy-done.8
  4.8 0.0 copy-start.9
  4.8 0.7 copy-done.9
  5.4 0.0 copy-start.11
  5.4 0.7 copy-done.11
  6.1 0.0 copy-start.13
  6.1 0.7 copy-done.13
  6.8 0.0 copy-start.14
  6.8 0.7 copy-done.14
  7.5 0.0 copy-start.4
  7.5 0.0 copy-start.6
  7.5 0.0 copy-start.10
  7.5 0.0 copy-start.12
  7.5 6.8 %first_kernel.1 = (f32[32,320]{1,0:T(8,128)S(1)}, f32[128,128]{1,0:T(8,128)}, s32[1,512]{1,0:T(1,128)S(1)}) custom-call(f32[32,320]{1,0:T(8,128)S(1)} %copy-done.5, bf16[32,320,320]{2,1,0:T(8,128)(2,1)S(1)} %copy-done, s32[1,512]{1,0:T(1,128)S(1)} %bitcast.28, s32[1,512]{1,0:T(1,128)S(1)} %bitcast.30, s32[1,512]{1,0:T(1,128)S(1)} %bitcast.32, ...), custom_call_target="tpu_custom_call" | custom-call | tf_op jit(solution)/shard_map/first_kernel/pallas_call | solution.py:358
  14.2 11.5 %all-to-all-start = ((f32[128,1,128]{2,1,0:T(1,128)}), f32[128,1,128]{2,1,0:T(1,128)S(1)}, u32[]{:S(2)}, u32[]{:S(2)}) async-start(f32[128,1,128]{2,1,0:T(1,128)} %bitcast.6), calls=%async_computation | async-start | bytes 131072 | tf_op jit(solution)/shard_map/all_to_all | solution.py:370
  25.7 0.0 copy-done.7
  25.8 0.0 copy-done.4
  25.8 0.0 copy-done.6
  25.8 0.0 copy-start.2
  25.8 2.1 %copy-done.2 = bf16[32,6,80,80]{3,2,1,0:T(8,128)(2,1)S(1)} copy-done((bf16[32,6,80,80]{3,2,1,0:T(8,128)(2,1)S(1)}, bf16[32,6,80,80]{3,2,1,0:T(8,128)(2,1)}, u32[]{:S(2)}) %copy-start.2) | copy-done | bytes 2457624
  27.9 5.1 %face_kernel.2 = (f32[32,320]{1,0:T(8,128)S(1)}, f32[32,80]{1,0:T(8,128)S(1)}, f32[32,80]{1,0:T(8,128)S(1)}) custom-call(f32[32,320]{1,0:T(8,128)S(1)} %get-tuple-element.20.z_ref, f32[32,320]{1,0:T(8,128)S(1)} %copy-done.6, bf16[32,480,80]{2,1,0:T(8,128)(2,1)S(1)} %bitcast.17, s32[6,32]{1,0:T(8,128)S(1)} %bitcast.23, bf16[480,320]{1,0:T(8,128)(2,1)S(1)} %copy-done.4), custom_call_target="tpu_custom_call" | custom-call | tf_op jit(solution)/shard_map/face_kernel/pallas_call | solution.py:358
  33.0 3.7 %collective-permute-start = (f32[32,80]{1,0:T(8,128)S(1)}, f32[32,80]{1,0:T(8,128)S(1)}, u32[]{:S(2)}, u32[]{:S(2)}) collective-permute-start(f32[32,80]{1,0:T(8,128)S(1)} %get-tuple-element.22), channel_id=1, source_target_pairs={{0,1},{1,2},{2,3},{3,4},{4,5},{5,6},{6,7},{7,8},{8,9},{9,10},{10,1... | collective-permute-start | bytes 30728 | tf_op jit(solution)/shard_map/ppermute | solution.py:406
  36.6 1.9 %collective-permute-start.1 = (f32[32,80]{1,0:T(8,128)S(1)}, f32[32,80]{1,0:T(8,128)S(1)}, u32[]{:S(2)}, u32[]{:S(2)}) collective-permute-start(f32[32,80]{1,0:T(8,128)S(1)} %get-tuple-element.23), channel_id=1, source_target_pairs={{1,0},{2,1},{3,2},{4,3},{5,4},{6,5},{7,6},{8,7},{9,8},{10,9},{11,1... | collective-permute-start | bytes 30728 | tf_op jit(solution)/shard_map/ppermute | solution.py:407
  38.6 0.0 collective-permute-done.low_ref
  38.6 3.1 %collective-permute-done.1.high_ref = f32[32,80]{1,0:T(8,128)S(1)} collective-permute-done((f32[32,80]{1,0:T(8,128)S(1)}, f32[32,80]{1,0:T(8,128)S(1)}, u32[]{:S(2)}, u32[]{:S(2)}) %collective-permute-start.1) | collective-permute-done | bytes 10272 | tf_op jit(solution)/shard_map/ppermute | solution.py:407
  41.7 0.5 arrived_kernel.2.base_ref
  42.2 0.0 all-to-all-done
  42.2 0.0 copy-done.15
  42.2 0.0 copy-done.10
  42.2 0.0 copy-done.12
  42.3 0.0 copy-start.1
  42.3 3.2 %copy-done.1 = bf16[32,320,320]{2,1,0:T(8,128)(2,1)S(1)} copy-done((bf16[32,320,320]{2,1,0:T(8,128)(2,1)S(1)}, bf16[32,320,320]{2,1,0:T(8,128)(2,1)}, u32[]{:S(2)}) %copy-start.1) | copy-done | bytes 6553624
  45.5 7.5 %second_kernel.1 = (f32[32,320]{1,0:T(8,128)S(1)}, f32[32,320]{1,0:T(8,128)S(1)}, f32[128,128]{1,0:T(8,128)}) custom-call(f32[32,320]{1,0:T(8,128)S(1)} %arrived_kernel.2.base_ref, f32[128,128]{1,0:T(8,128)S(1)} %bitcast.19, f32[32,320]{1,0:T(8,128)S(1)} %copy-done.6, bf16[32,320,320]{2,1,0:T(8,128)(2,1)S(1)} %copy-done.1, s32[1,512]{1,0:T(1,128)S(1)} %bitcast.29, ...), custom_call_target="tpu_custom_call" | custom-call | tf_op jit(solution)/shard_map/second_kernel/pallas_call | solution.py:358
  53.0 10.2 %all-to-all-start.1 = ((f32[128,1,128]{2,1,0:T(1,128)}), f32[128,1,128]{2,1,0:T(1,128)S(1)}, u32[]{:S(2)}, u32[]{:S(2)}) async-start(f32[128,1,128]{2,1,0:T(1,128)} %bitcast.9), calls=%async_computation.1 | async-start | bytes 131072 | tf_op jit(solution)/shard_map/all_to_all | solution.py:370
  63.2 0.0 copy-start.3
  63.2 2.1 %copy-done.3 = bf16[32,6,80,80]{3,2,1,0:T(8,128)(2,1)S(1)} copy-done((bf16[32,6,80,80]{3,2,1,0:T(8,128)(2,1)S(1)}, bf16[32,6,80,80]{3,2,1,0:T(8,128)(2,1)}, u32[]{:S(2)}) %copy-start.3) | copy-done | bytes 2457624
  65.3 5.1 %face_kernel.3 = (f32[32,320]{1,0:T(8,128)S(1)}, f32[32,80]{1,0:T(8,128)S(1)}, f32[32,80]{1,0:T(8,128)S(1)}) custom-call(f32[32,320]{1,0:T(8,128)S(1)} %get-tuple-element.26.z_ref, f32[32,320]{1,0:T(8,128)S(1)} %get-tuple-element.27.x_ref.u_ref, bf16[32,480,80]{2,1,0:T(8,128)(2,1)S(1)} %bitcast.18, s32[6,32]{1,0:T(8,128)S(1)} %bitcast.25, ...), custom_call_target="tpu_custom_call" | custom-call | tf_op jit(solution)/shard_map/face_kernel/pallas_call | solution.py:358
  70.4 3.7 %collective-permute-start.2 = (f32[32,80]{1,0:T(8,128)S(1)}, f32[32,80]{1,0:T(8,128)S(1)}, u32[]{:S(2)}, u32[]{:S(2)}) collective-permute-start(f32[32,80]{1,0:T(8,128)S(1)} %get-tuple-element.29), channel_id=1, source_target_pairs={{0,1},{1,2},{2,3},{3,4},{4,5},{5,6},{6,7},{7,8},{8,9},{9,10},{10,1... | collective-permute-start | bytes 30728 | tf_op jit(solution)/shard_map/ppermute | solution.py:406
  74.0 1.9 %collective-permute-start.3 = (f32[32,80]{1,0:T(8,128)S(1)}, f32[32,80]{1,0:T(8,128)S(1)}, u32[]{:S(2)}, u32[]{:S(2)}) collective-permute-start(f32[32,80]{1,0:T(8,128)S(1)} %get-tuple-element.30), channel_id=1, source_target_pairs={{1,0},{2,1},{3,2},{4,3},{5,4},{6,5},{7,6},{8,7},{9,8},{10,9},{11,1... | collective-permute-start | bytes 30728 | tf_op jit(solution)/shard_map/ppermute | solution.py:407
  76.0 0.0 collective-permute-done.2.low_ref
  76.0 3.1 %collective-permute-done.3.high_ref = f32[32,80]{1,0:T(8,128)S(1)} collective-permute-done((f32[32,80]{1,0:T(8,128)S(1)}, f32[32,80]{1,0:T(8,128)S(1)}, u32[]{:S(2)}, u32[]{:S(2)}) %collective-permute-start.3) | collective-permute-done | bytes 10272 | tf_op jit(solution)/shard_map/ppermute | solution.py:407
  79.1 0.5 arrived_kernel.3.base_ref
  79.6 0.0 all-to-all-done.1
  79.6 0.7 third_kernel.1
  80.4 19.4 %all_to_all.15 = f32[128,1,128]{2,1,0:T(1,128)S(1)} all-to-all(f32[128,1,128]{2,1,0:T(1,128)S(1)} %bitcast.27), channel_id=1, replica_groups=mesh['grp'=4,'dom'=32] {'grp','dom'}, dimensions={0} | all-to-all | bytes 131072 | tf_op jit(solution)/shard_map/all_to_all | solution.py:370
  99.8 1.1 %last_kernel.1 = f32[32,320]{1,0:T(8,128)} custom-call(f32[128,128]{1,0:T(8,128)S(1)} %bitcast.22, f32[8,128]{1,0:T(8,128)S(1)} %get-tuple-element.33.known_ref, f32[32,320]{1,0:T(8,128)S(1)} %copy-done.6, f32[32,320]{1,0:T(8,128)S(1)} %get-tuple-element.34.rest_ref), custom_call_target="tpu_custom_call" | custom-call | tf_op jit(solution)/shard_map/last_kernel/pallas_call | solution.py:358
Async XLA Ops:
  0.0 42.2 %copy-start.15 = (s32[1,4]{1,0:T(1,128)S(1)}, s32[1,4]{1,0:T(1,128)}, u32[]{:S(2)}) copy-start(s32[1,4]{1,0:T(1,128)} %count_ref.3) | copy-start | bytes 52
  0.0 25.7 %copy-start.7 = (s32[32,6]{0,1:T(8,128)S(1)}, s32[32,6]{0,1:T(8,128)}, u32[]{:S(2)}) copy-start(s32[32,6]{0,1:T(8,128)} %param.13) | copy-start | bytes 2308
  0.0 3.3 %copy-start = (bf16[32,320,320]{2,1,0:T(8,128)(2,1)S(1)}, bf16[32,320,320]{2,1,0:T(8,128)(2,1)}, u32[]{:S(2)}) copy-start(bf16[32,320,320]{2,1,0:T(8,128)(2,1)} %blocks_ref.3) | copy-start | bytes 19660804
  3.3 0.8 copy-start.5
  4.1 0.7 copy-start.8
  4.8 0.7 copy-start.9
  5.4 0.7 copy-start.11
  6.1 0.7 copy-start.13
  6.8 0.7 copy-start.14
  7.5 18.3 %copy-start.4 = (bf16[480,320]{1,0:T(8,128)(2,1)S(1)}, bf16[480,320]{1,0:T(8,128)(2,1)}, u32[]{:S(2)}) copy-start(bf16[480,320]{1,0:T(8,128)(2,1)} %constant.2.clone.spread_ref) | copy-start | bytes 921604
  7.5 18.3 %copy-start.6 = (f32[32,320]{1,0:T(8,128)S(1)}, f32[32,320]{1,0:T(8,128)}, u32[]{:S(2)}) copy-start(f32[32,320]{1,0:T(8,128)} %b_ref.5) | copy-start | bytes 122884
  7.5 34.8 %copy-start.10 = (s32[512]{0:T(512)S(1)}, s32[512]{0:T(512)}, u32[]{:S(2)}) copy-start(s32[512]{0:T(512)} %param.14) | copy-start | bytes 6148
  7.5 34.8 %copy-start.12 = (s32[512,1]{0,1:T(1,128)S(1)}, s32[512,1]{0,1:T(1,128)}, u32[]{:S(2)}) copy-start(s32[512,1]{0,1:T(1,128)} %param.15) | copy-start | bytes 6148
  14.2 28.0 %all-to-all-start = ((f32[128,1,128]{2,1,0:T(1,128)}), f32[128,1,128]{2,1,0:T(1,128)S(1)}, u32[]{:S(2)}, u32[]{:S(2)}) async-start(f32[128,1,128]{2,1,0:T(1,128)} %bitcast.6), calls=%async_computation | async-start | bytes 131072 | tf_op jit(solution)/shard_map/all_to_all | solution.py:370
  25.8 2.1 %copy-start.2 = (bf16[32,6,80,80]{3,2,1,0:T(8,128)(2,1)S(1)}, bf16[32,6,80,80]{3,2,1,0:T(8,128)(2,1)}, u32[]{:S(2)}) copy-start(bf16[32,6,80,80]{3,2,1,0:T(8,128)(2,1)} %param.12) | copy-start | bytes 7372804
  33.0 5.6 %collective-permute-start = (f32[32,80]{1,0:T(8,128)S(1)}, f32[32,80]{1,0:T(8,128)S(1)}, u32[]{:S(2)}, u32[]{:S(2)}) collective-permute-start(f32[32,80]{1,0:T(8,128)S(1)} %get-tuple-element.22), channel_id=1, source_target_pairs={{0,1},{1,2},{2,3},{3,4},{4,5},{5,6},{6,7},{7,8},{8,9},{9,10},{10,1... | collective-permute-start | bytes 30728 | tf_op jit(solution)/shard_map/ppermute | solution.py:406
  36.6 5.1 %collective-permute-start.1 = (f32[32,80]{1,0:T(8,128)S(1)}, f32[32,80]{1,0:T(8,128)S(1)}, u32[]{:S(2)}, u32[]{:S(2)}) collective-permute-start(f32[32,80]{1,0:T(8,128)S(1)} %get-tuple-element.23), channel_id=1, source_target_pairs={{1,0},{2,1},{3,2},{4,3},{5,4},{6,5},{7,6},{8,7},{9,8},{10,9},{11,1... | collective-permute-start | bytes 30728 | tf_op jit(solution)/shard_map/ppermute | solution.py:407
  42.3 3.2 %copy-start.1 = (bf16[32,320,320]{2,1,0:T(8,128)(2,1)S(1)}, bf16[32,320,320]{2,1,0:T(8,128)(2,1)}, u32[]{:S(2)}) copy-start(bf16[32,320,320]{2,1,0:T(8,128)(2,1)} %blocks_ref.3) | copy-start | bytes 19660804
  53.0 26.6 %all-to-all-start.1 = ((f32[128,1,128]{2,1,0:T(1,128)}), f32[128,1,128]{2,1,0:T(1,128)S(1)}, u32[]{:S(2)}, u32[]{:S(2)}) async-start(f32[128,1,128]{2,1,0:T(1,128)} %bitcast.9), calls=%async_computation.1 | async-start | bytes 131072 | tf_op jit(solution)/shard_map/all_to_all | solution.py:370
  63.2 2.1 %copy-start.3 = (bf16[32,6,80,80]{3,2,1,0:T(8,128)(2,1)S(1)}, bf16[32,6,80,80]{3,2,1,0:T(8,128)(2,1)}, u32[]{:S(2)}) copy-start(bf16[32,6,80,80]{3,2,1,0:T(8,128)(2,1)} %param.12) | copy-start | bytes 7372804
  70.4 5.6 %collective-permute-start.2 = (f32[32,80]{1,0:T(8,128)S(1)}, f32[32,80]{1,0:T(8,128)S(1)}, u32[]{:S(2)}, u32[]{:S(2)}) collective-permute-start(f32[32,80]{1,0:T(8,128)S(1)} %get-tuple-element.29), channel_id=1, source_target_pairs={{0,1},{1,2},{2,3},{3,4},{4,5},{5,6},{6,7},{7,8},{8,9},{9,10},{10,1... | collective-permute-start | bytes 30728 | tf_op jit(solution)/shard_map/ppermute | solution.py:406
  74.0 5.1 %collective-permute-start.3 = (f32[32,80]{1,0:T(8,128)S(1)}, f32[32,80]{1,0:T(8,128)S(1)}, u32[]{:S(2)}, u32[]{:S(2)}) collective-permute-start(f32[32,80]{1,0:T(8,128)S(1)} %get-tuple-element.30), channel_id=1, source_target_pairs={{1,0},{2,1},{3,2},{4,3},{5,4},{6,5},{7,6},{8,7},{9,8},{10,9},{11,1... | collective-permute-start | bytes 30728 | tf_op jit(solution)/shard_map/ppermute | solution.py:407

commit v2 on v1

--- a/solution.py
+++ b/solution.py
@@ -21,7 +21,7 @@
 EPS = 1e-06
 F32 = jnp.float32
 BF16 = jnp.bfloat16
-VMEM_LIMIT = 40 * 1024 * 1024
+VMEM_LIMIT = 24 * 1024 * 1024
 
 
 def face_table():
@@ -186,12 +186,24 @@
 
 
 def first_kernel(
-    x_ref, blocks_ref, node_ref, owner_ref, elem_ref, coord_ref, count_ref,
-    z_ref, pay_ref, rank_ref, buf, sems,
+    x_hbm, blocks_ref, node_hbm, owner_hbm, elem_hbm, coord_hbm, count_hbm,
+    z_ref, pay_ref, rank_ref,
+    x_ref, node_ref, owner_ref, elem_ref, coord_ref, count_ref, small_sems, buf, sems,
 ):
+    small = [
+        pltpu.make_async_copy(src, dst, small_sems.at[i])
+        for i, (src, dst) in enumerate(
+            [
+                (owner_hbm, owner_ref), (x_hbm, x_ref), (node_hbm, node_ref),
+                (elem_hbm, elem_ref), (coord_hbm, coord_ref), (count_hbm, count_ref),
+            ]
+        )
+    ]
     copies = stream(blocks_ref, buf, sems)
-    for one in copies:
+    for one in small + copies:
         one.start()
+    for one in small:
+        one.wait()
     hot = owner_one_hot(owner_ref[...])
     hot16 = hot.astype(BF16)
     earlier = (iota((RPTS, RPTS), 0) < iota((RPTS, RPTS), 1)).astype(F32).astype(BF16)
@@ -208,7 +220,7 @@
 
 def face_kernel(
     z_ref, x_ref, jac_ref, nbr_ref, spread_ref,
-    base_ref, low_ref, high_ref, traces, outs, buf, sems,
+    base_ref, first_ref, second_ref, traces, outs, buf, sems,
 ):
     copies = stream(jac_ref, buf, sems)
     for one in copies:
@@ -236,8 +248,10 @@
     hi, lo = hi.astype(BF16), lo.astype(BF16)
     local_hot, iface_hot = neighbour_one_hots(nbr_ref[...])
     outgoing = dot(iface_hot, hi) + dot(iface_hot, lo)
-    low_ref[...] = outgoing[:E]
-    high_ref[...] = outgoing[E:]
+    odd = lax.axis_index("dom") % 2 == 1
+    low, high = outgoing[:E], outgoing[E:]
+    first_ref[...] = jnp.where(odd, low, high)
+    second_ref[...] = jnp.where(odd, high, low)
     incoming = dot_tn(local_hot, hi) + dot_tn(local_hot, lo)
     base_ref[...] = x_ref[...] - spread_faces(incoming, spread_ref)
 
@@ -264,8 +278,11 @@
     return acc[:E] + acc[E:]
 
 
-def arrived_kernel(base_ref, low_ref, high_ref, nbr_ref, spread_ref, out_ref):
-    hi, lo = split(jnp.concatenate([low_ref[...], high_ref[...]], axis=0))
+def arrived_kernel(base_ref, first_ref, second_ref, nbr_ref, spread_ref, out_ref):
+    odd = lax.axis_index("dom") % 2 == 1
+    first, second = first_ref[...], second_ref[...]
+    low, high = jnp.where(odd, first, second), jnp.where(odd, second, first)
+    hi, lo = split(jnp.concatenate([low, high], axis=0))
     _, iface_hot = neighbour_one_hots(nbr_ref[...])
     incoming = dot_tn(iface_hot, hi.astype(BF16)) + dot_tn(iface_hot, lo.astype(BF16))
     out_ref[...] = base_ref[...] - spread_faces(incoming, spread_ref)
@@ -351,7 +368,17 @@
 
 VM = pl.BlockSpec(memory_space=pltpu.VMEM)
 SM = pl.BlockSpec(memory_space=pltpu.SMEM)
-ANY = pl.BlockSpec(memory_space=pl.ANY)
+
+
+HBM = pl.BlockSpec(memory_space=pltpu.HBM)
+
+
+def swaps(start, ends):
+    return [pair for i in range(start, ends, 2) for pair in ((i, i + 1), (i + 1, i))]
+
+
+def in_hbm(x):
+    return pltpu.with_memory_space_constraint(x, pltpu.HBM)
 
 
 def call(kernel, in_specs, outs, scratch, *args):
@@ -382,18 +409,21 @@
     elem = donor_elem.reshape(1, RPTS)
     spread = jnp.asarray(spread_matrix(), BF16)
     ends = lax.axis_size("dom") - 1
-    upward = [(i, i + 1) for i in range(ends)]
-    downward = [(i + 1, i) for i in range(ends)]
+    even_pairs = swaps(0, ends)
+    odd_pairs = swaps(1, ends)
     full = ((E, BLOCK), F32)
     table = ((PEERS, PEERS), F32)
     half = ((E, FACEW), F32)
+    row = pltpu.VMEM((1, RPTS), jnp.int32)
     block_scratch = [pltpu.VMEM((E, BLOCK, BLOCK), BF16), pltpu.SemaphoreType.DMA((CHUNKS,))]
+    blocks = in_hbm(block_inv)
+    jac = in_hbm(jac)
     rows_scratch = pltpu.VMEM((8 * (13 + 2 * VARS), PEERS), F32)
 
     def faces(z, x):
-        base, low, high = call(
+        base, first, second = call(
             face_kernel,
-            [VM, VM, ANY, VM, VM],
+            [VM, VM, HBM, VM, VM],
             [full, half, half],
             [
                 pltpu.VMEM((2 * E, 6 * FACEW), F32),
@@ -403,27 +433,31 @@
             ],
             z, x, jac, nbr, spread,
         )
-        from_lower = lax.ppermute(high, "dom", upward)
-        from_upper = lax.ppermute(low, "dom", downward)
-        return call(
-            arrived_kernel, [VM] * 5, [full], [], base, from_lower, from_upper, nbr, spread
-        )[0]
+        second = lax.ppermute(second, "dom", odd_pairs)
+        first = lax.ppermute(first, "dom", even_pairs)
+        return call(arrived_kernel, [VM] * 5, [full], [], base, first, second, nbr, spread)[0]
 
     z1, pay1, rank = call(
         first_kernel,
-        [VM, ANY, VM, VM, VM, VM, SM],
+        [HBM] * 7,
         [full, table, ((1, RPTS), jnp.int32)],
-        block_scratch,
-        grad_rhs, block_inv, node, owner, elem, donor_coords, recv_counts,
+        [
+            pltpu.VMEM((E, BLOCK), F32), row, row, row, pltpu.VMEM((3, RPTS), F32),
+            pltpu.SMEM((1, 4), jnp.int32),
+            pltpu.SemaphoreType.DMA((6,)),
+        ]
+        + block_scratch,
+        in_hbm(grad_rhs), blocks, in_hbm(node), in_hbm(owner), in_hbm(elem),
+        in_hbm(donor_coords), in_hbm(recv_counts),
     )
     got1 = exchange(pay1)
     base1 = faces(z1, grad_rhs)
     u, z2, pay2 = call(
         second_kernel,
-        [VM, VM, VM, ANY, VM, VM, VM, SM],
+        [VM, VM, VM, HBM, VM, VM, VM, SM],
         [full, full, table],
         [rows_scratch] + block_scratch,
-        base1, got1, grad_rhs, block_inv, node, owner, rank, recv_counts,
+        base1, got1, grad_rhs, blocks, node, owner, rank, recv_counts,
     )
     got2 = exchange(pay2)
     base2 = faces(z2, u)

time: 101 us -> 76.6 us (0.76)
  local copies, waits for them, and re-layouts: 14.9 us -> 0.02 us
  Pallas kernels: 27.2 us -> 21.3 us
  starting transfers between devices: 32.9 us -> 29.9 us
  waiting for transfers between devices: 6.25 us -> 5.19 us
    unnamed x32 -> x12, local copies, waits for them, and re-layouts: 14.9 us -> 0.02 us
    pallas_call x8, Pallas kernels: 27.2 us -> 21.3 us  [call(): pl.pallas_call(kernel, in_specs=in_specs, out_specs=[VM] * len(outs), out...]
    ppermute x4, starting transfers between devices: 11.2 us -> 7.76 us  [the longest x2 5.46 us: faces(): second = lax.ppermute(second, 'dom', odd_pairs)]
    ppermute x4, waiting for transfers between devices: 6.24 us -> 5.19 us  [the longest x2 5.18 us: faces(): second = lax.ppermute(second, 'dom', odd_pairs)]
  transfers between devices with their start and end apart: 6 -> 6, of which waited for: 2 -> 2; matrix products, arithmetic and copies ran while one was open for 0% -> 0% of each run, Pallas kernels for 11% -> 10%
where the time goes in v2:
time: 76.6 us; the launch traced here: 76.4 us
  starting transfers between devices  29.9 us (39%)
  Pallas kernels  21.3 us (28%)
  blocking collectives  19.8 us (26%)
  waiting for transfers between devices  5.19 us (7%)
    all_to_all x2, starting transfers between devices, exchange(): lax.all_to_all(table.reshape(PEERS, 1, PEERS), AXES, split_axis=0, concat...  22.1 us
    pallas_call x8, Pallas kernels, call(): pl.pallas_call(kernel, in_specs=in_specs, out_specs=[VM] * len(outs), out...  21.3 us
    all_to_all x1, blocking collectives, exchange(): lax.all_to_all(table.reshape(PEERS, 1, PEERS), AXES, split_axis=0, concat...  19.8 us
    ppermute x2, starting transfers between devices, faces(): second = lax.ppermute(second, 'dom', odd_pairs)  5.46 us
    ppermute x2, waiting for transfers between devices, faces(): second = lax.ppermute(second, 'dom', odd_pairs)  5.18 us
    ppermute x2, starting transfers between devices, faces(): first = lax.ppermute(first, 'dom', even_pairs)  2.3 us
  transfers between devices with their start and end apart: 6, of which 2 were waited for; matrix products, arithmetic and copies ran while one was open for 0% of the time, Pallas kernels for 10%

profile of v2, /device:TPU:1, one launch (start us, length us, event | category | flops | bytes accessed | tf_op | source)
XLA Modules:
  0.0 76.4 jit_solution(17242102270279634213)
XLA Ops:
  0.0 0.0 copy-start
  0.0 0.0 copy-start.1
  0.0 0.0 copy-start.5
  0.0 0.0 copy-start.4
  0.0 0.0 copy-start.3
  0.0 0.0 copy-start.2
  0.0 6.4 %first_kernel.1 = (f32[32,320]{1,0:T(8,128)S(1)}, f32[128,128]{1,0:T(8,128)}, s32[1,512]{1,0:T(1,128)S(1)}) custom-call(f32[32,320]{1,0:T(8,128)} %b_ref.5, bf16[32,320,320]{2,1,0:T(8,128)(2,1)} %blocks_ref.3, s32[1,512]{1,0:T(1,128)} %bitcast.26, s32[1,512]{1,0:T(1,128)} %bitcast.28, s32[1,512]{1,0:T(1,128)} %bitcast.32, f32[3,512]{1,0:T(4,128)} %coord_hbm.1, ...), custom_call_target="tpu_custom_call" | custom-call | tf_op jit(solution)/shard_map/first_kernel/pallas_call | solution.py:385
  6.4 11.5 %all-to-all-start = ((f32[128,1,128]{2,1,0:T(1,128)}), f32[128,1,128]{2,1,0:T(1,128)S(1)}, u32[]{:S(2)}, u32[]{:S(2)}) async-start(f32[128,1,128]{2,1,0:T(1,128)} %bitcast.6), calls=%async_computation | async-start | bytes 131072 | tf_op jit(solution)/shard_map/all_to_all | solution.py:397
  17.9 0.0 copy-done
  17.9 0.0 copy-done.1
  17.9 0.0 copy-done.2
  18.0 3.3 %face_kernel.2 = (f32[32,320]{1,0:T(8,128)S(1)}, f32[32,80]{1,0:T(8,128)S(1)}, f32[32,80]{1,0:T(8,128)S(1)}) custom-call(f32[32,320]{1,0:T(8,128)S(1)} %get-tuple-element.20.z_ref, f32[32,320]{1,0:T(8,128)S(1)} %copy-done.1, bf16[32,480,80]{2,1,0:T(8,128)(2,1)} %bitcast.30, s32[6,32]{1,0:T(8,128)S(1)} %bitcast.21, bf16[480,320]{1,0:T(8,128)(2,1)S(1)} %copy-done), custom_call_target="tpu_custom_call" | custom-call | tf_op jit(solution)/shard_map/face_kernel/pallas_call | solution.py:385
  21.3 1.1 %collective-permute-start = (f32[32,80]{1,0:T(8,128)S(1)}, f32[32,80]{1,0:T(8,128)S(1)}, u32[]{:S(2)}, u32[]{:S(2)}) collective-permute-start(f32[32,80]{1,0:T(8,128)S(1)} %get-tuple-element.22), channel_id=1, source_target_pairs={{0,1},{1,0},{2,3},{3,2},{4,5},{5,4},{6,7},{7,6},{8,9},{9,8},{10,11... | collective-permute-start | bytes 30728 | tf_op jit(solution)/shard_map/ppermute | solution.py:437
  22.4 2.7 %collective-permute-start.1 = (f32[32,80]{1,0:T(8,128)S(1)}, f32[32,80]{1,0:T(8,128)S(1)}, u32[]{:S(2)}, u32[]{:S(2)}) collective-permute-start(f32[32,80]{1,0:T(8,128)S(1)} %get-tuple-element.23), channel_id=1, source_target_pairs={{1,2},{2,1},{3,4},{4,3},{5,6},{6,5},{7,8},{8,7},{9,10},{10,9},{11,... | collective-permute-start | bytes 30728 | tf_op jit(solution)/shard_map/ppermute | solution.py:436
  25.2 0.0 collective-permute-done.first_ref
  25.2 2.6 %collective-permute-done.1.second_ref = f32[32,80]{1,0:T(8,128)S(1)} collective-permute-done((f32[32,80]{1,0:T(8,128)S(1)}, f32[32,80]{1,0:T(8,128)S(1)}, u32[]{:S(2)}, u32[]{:S(2)}) %collective-permute-start.1) | collective-permute-done | bytes 10272 | tf_op jit(solution)/shard_map/ppermute | solution.py:436
  27.8 0.5 arrived_kernel.2.base_ref
  28.3 0.0 all-to-all-done
  28.3 0.0 copy-done.5
  28.3 0.0 copy-done.4
  28.3 0.0 copy-done.3
  28.3 5.5 %second_kernel.1 = (f32[32,320]{1,0:T(8,128)S(1)}, f32[32,320]{1,0:T(8,128)S(1)}, f32[128,128]{1,0:T(8,128)}) custom-call(f32[32,320]{1,0:T(8,128)S(1)} %arrived_kernel.2.base_ref, f32[128,128]{1,0:T(8,128)S(1)} %bitcast.17, f32[32,320]{1,0:T(8,128)S(1)} %copy-done.1, bf16[32,320,320]{2,1,0:T(8,128)(2,1)} %blocks_ref.3, s32[1,512]{1,0:T(1,128)S(1)} %bitcast.27, ...), custom_call_target="tpu_custom_call" | custom-call | tf_op jit(solution)/shard_map/second_kernel/pallas_call | solution.py:385
  33.8 10.6 %all-to-all-start.1 = ((f32[128,1,128]{2,1,0:T(1,128)}), f32[128,1,128]{2,1,0:T(1,128)S(1)}, u32[]{:S(2)}, u32[]{:S(2)}) async-start(f32[128,1,128]{2,1,0:T(1,128)} %bitcast.9), calls=%async_computation.1 | async-start | bytes 131072 | tf_op jit(solution)/shard_map/all_to_all | solution.py:397
  44.4 3.3 %face_kernel.3 = (f32[32,320]{1,0:T(8,128)S(1)}, f32[32,80]{1,0:T(8,128)S(1)}, f32[32,80]{1,0:T(8,128)S(1)}) custom-call(f32[32,320]{1,0:T(8,128)S(1)} %get-tuple-element.26.z_ref, f32[32,320]{1,0:T(8,128)S(1)} %get-tuple-element.27.x_ref.u_ref, bf16[32,480,80]{2,1,0:T(8,128)(2,1)} %bitcast.31, s32[6,32]{1,0:T(8,128)S(1)} %bitcast.23, ...), custom_call_target="tpu_custom_call" | custom-call | tf_op jit(solution)/shard_map/face_kernel/pallas_call | solution.py:385
  47.7 1.1 %collective-permute-start.2 = (f32[32,80]{1,0:T(8,128)S(1)}, f32[32,80]{1,0:T(8,128)S(1)}, u32[]{:S(2)}, u32[]{:S(2)}) collective-permute-start(f32[32,80]{1,0:T(8,128)S(1)} %get-tuple-element.29), channel_id=1, source_target_pairs={{0,1},{1,0},{2,3},{3,2},{4,5},{5,4},{6,7},{7,6},{8,9},{9,8},{10,11... | collective-permute-start | bytes 30728 | tf_op jit(solution)/shard_map/ppermute | solution.py:437
  48.9 2.7 %collective-permute-start.3 = (f32[32,80]{1,0:T(8,128)S(1)}, f32[32,80]{1,0:T(8,128)S(1)}, u32[]{:S(2)}, u32[]{:S(2)}) collective-permute-start(f32[32,80]{1,0:T(8,128)S(1)} %get-tuple-element.30), channel_id=1, source_target_pairs={{1,2},{2,1},{3,4},{4,3},{5,6},{6,5},{7,8},{8,7},{9,10},{10,9},{11,... | collective-permute-start | bytes 30728 | tf_op jit(solution)/shard_map/ppermute | solution.py:436
  51.6 0.0 collective-permute-done.2.first_ref
  51.6 2.6 %collective-permute-done.3.second_ref = f32[32,80]{1,0:T(8,128)S(1)} collective-permute-done((f32[32,80]{1,0:T(8,128)S(1)}, f32[32,80]{1,0:T(8,128)S(1)}, u32[]{:S(2)}, u32[]{:S(2)}) %collective-permute-start.3) | collective-permute-done | bytes 10272 | tf_op jit(solution)/shard_map/ppermute | solution.py:436
  54.2 0.5 arrived_kernel.3.base_ref
  54.8 0.0 all-to-all-done.1
  54.8 0.7 third_kernel.1
  55.5 19.8 %all_to_all.15 = f32[128,1,128]{2,1,0:T(1,128)S(1)} all-to-all(f32[128,1,128]{2,1,0:T(1,128)S(1)} %bitcast.25), channel_id=1, replica_groups=mesh['grp'=4,'dom'=32] {'grp','dom'}, dimensions={0} | all-to-all | bytes 131072 | tf_op jit(solution)/shard_map/all_to_all | solution.py:397
  75.3 1.1 %last_kernel.1 = f32[32,320]{1,0:T(8,128)} custom-call(f32[128,128]{1,0:T(8,128)S(1)} %bitcast.20, f32[8,128]{1,0:T(8,128)S(1)} %get-tuple-element.33.known_ref, f32[32,320]{1,0:T(8,128)S(1)} %copy-done.1, f32[32,320]{1,0:T(8,128)S(1)} %get-tuple-element.34.rest_ref), custom_call_target="tpu_custom_call" | custom-call | tf_op jit(solution)/shard_map/last_kernel/pallas_call | solution.py:385
Async XLA Ops:
  0.0 17.9 %copy-start = (bf16[480,320]{1,0:T(8,128)(2,1)S(1)}, bf16[480,320]{1,0:T(8,128)(2,1)}, u32[]{:S(2)}) copy-start(bf16[480,320]{1,0:T(8,128)(2,1)} %constant.2.clone.spread_ref) | copy-start | bytes 921604
  0.0 17.9 %copy-start.1 = (f32[32,320]{1,0:T(8,128)S(1)}, f32[32,320]{1,0:T(8,128)}, u32[]{:S(2)}) copy-start(f32[32,320]{1,0:T(8,128)} %b_ref.5) | copy-start | bytes 122884
  0.0 28.3 %copy-start.5 = (s32[1,4]{1,0:T(1,128)S(1)}, s32[1,4]{1,0:T(1,128)}, u32[]{:S(2)}) copy-start(s32[1,4]{1,0:T(1,128)} %count_ref.1) | copy-start | bytes 52
  0.0 28.3 %copy-start.4 = (s32[512,1]{0,1:T(1,128)S(1)}, s32[512,1]{0,1:T(1,128)}, u32[]{:S(2)}) copy-start(s32[512,1]{0,1:T(1,128)} %param.15) | copy-start | bytes 6148
  0.0 28.3 %copy-start.3 = (s32[512]{0:T(512)S(1)}, s32[512]{0:T(512)}, u32[]{:S(2)}) copy-start(s32[512]{0:T(512)} %param.14) | copy-start | bytes 6148
  0.0 17.9 %copy-start.2 = (s32[32,6]{0,1:T(8,128)S(1)}, s32[32,6]{0,1:T(8,128)}, u32[]{:S(2)}) copy-start(s32[32,6]{0,1:T(8,128)} %param.13) | copy-start | bytes 2308
  6.4 21.9 %all-to-all-start = ((f32[128,1,128]{2,1,0:T(1,128)}), f32[128,1,128]{2,1,0:T(1,128)S(1)}, u32[]{:S(2)}, u32[]{:S(2)}) async-start(f32[128,1,128]{2,1,0:T(1,128)} %bitcast.6), calls=%async_computation | async-start | bytes 131072 | tf_op jit(solution)/shard_map/all_to_all | solution.py:397
  21.3 3.9 %collective-permute-start = (f32[32,80]{1,0:T(8,128)S(1)}, f32[32,80]{1,0:T(8,128)S(1)}, u32[]{:S(2)}, u32[]{:S(2)}) collective-permute-start(f32[32,80]{1,0:T(8,128)S(1)} %get-tuple-element.22), channel_id=1, source_target_pairs={{0,1},{1,0},{2,3},{3,2},{4,5},{5,4},{6,7},{7,6},{8,9},{9,8},{10,11... | collective-permute-start | bytes 30728 | tf_op jit(solution)/shard_map/ppermute | solution.py:437
  22.4 5.3 %collective-permute-start.1 = (f32[32,80]{1,0:T(8,128)S(1)}, f32[32,80]{1,0:T(8,128)S(1)}, u32[]{:S(2)}, u32[]{:S(2)}) collective-permute-start(f32[32,80]{1,0:T(8,128)S(1)} %get-tuple-element.23), channel_id=1, source_target_pairs={{1,2},{2,1},{3,4},{4,3},{5,6},{6,5},{7,8},{8,7},{9,10},{10,9},{11,... | collective-permute-start | bytes 30728 | tf_op jit(solution)/shard_map/ppermute | solution.py:436
  33.8 21.0 %all-to-all-start.1 = ((f32[128,1,128]{2,1,0:T(1,128)}), f32[128,1,128]{2,1,0:T(1,128)S(1)}, u32[]{:S(2)}, u32[]{:S(2)}) async-start(f32[128,1,128]{2,1,0:T(1,128)} %bitcast.9), calls=%async_computation.1 | async-start | bytes 131072 | tf_op jit(solution)/shard_map/all_to_all | solution.py:397
  47.7 3.9 %collective-permute-start.2 = (f32[32,80]{1,0:T(8,128)S(1)}, f32[32,80]{1,0:T(8,128)S(1)}, u32[]{:S(2)}, u32[]{:S(2)}) collective-permute-start(f32[32,80]{1,0:T(8,128)S(1)} %get-tuple-element.29), channel_id=1, source_target_pairs={{0,1},{1,0},{2,3},{3,2},{4,5},{5,4},{6,7},{7,6},{8,9},{9,8},{10,11... | collective-permute-start | bytes 30728 | tf_op jit(solution)/shard_map/ppermute | solution.py:437
  48.9 5.3 %collective-permute-start.3 = (f32[32,80]{1,0:T(8,128)S(1)}, f32[32,80]{1,0:T(8,128)S(1)}, u32[]{:S(2)}, u32[]{:S(2)}) collective-permute-start(f32[32,80]{1,0:T(8,128)S(1)} %get-tuple-element.30), channel_id=1, source_target_pairs={{1,2},{2,1},{3,4},{4,3},{5,6},{6,5},{7,8},{8,7},{9,10},{10,9},{11,... | collective-permute-start | bytes 30728 | tf_op jit(solution)/shard_map/ppermute | solution.py:436

commit v3 on v2

--- a/solution.py
+++ b/solution.py
@@ -15,7 +15,10 @@
 PEERS = 128
 CAP = 8
 RPTS = 512
-CHUNKS = 8
+BLOCK_CHUNKS = (16, 16)
+START_JAC = 0
+AHEAD = 2
+JAC_CHUNKS = (16, 16)
 SCALAR_LANE = 96
 GLL = (-1.0, -0.4472135954999579, 0.4472135954999579, 1.0)
 EPS = 1e-06
@@ -64,18 +67,31 @@
     return jnp.sum(jnp.sum(x, axis=0, keepdims=True), axis=1, keepdims=True)
 
 
-def stream(src, dst, sems):
-    step = src.shape[0] // CHUNKS
-    return [
-        pltpu.make_async_copy(
-            src.at[pl.ds(c * step, step)], dst.at[pl.ds(c * step, step)], sems.at[c]
-        )
-        for c in range(CHUNKS)
-    ]
-
-
-def block_solve(x, blocks, copies):
-    step = E // CHUNKS
+def stream(src, dst, sems, sizes):
+    copies = {}
+    at = 0
+    for c, size in enumerate(sizes):
+        copies[at] = pltpu.make_async_copy(src.at[pl.ds(at, size)], dst.at[pl.ds(at, size)], sems.at[c])
+        at += size
+    return copies
+
+
+def start_order(blocks, jac):
+    order = list(blocks.values())
+    for one in order[:AHEAD]:
+        one.start()
+    then = {at: [] for at in blocks}
+    for at, one in zip(blocks, order[AHEAD:]):
+        then[at].append(one)
+    if START_JAC < 0:
+        for one in jac.values():
+            one.start()
+    else:
+        then[START_JAC] += list(jac.values())
+    return then
+
+
+def block_solve(x, blocks, copies, then):
     row = iota((16, BLOCK), 0) % 8
     parts = []
     for g in range(E // 8):
@@ -84,33 +100,39 @@
         acc = None
         for k in range(8):
             e = 8 * g + k
-            if e % step == 0:
-                copies[e // step].wait()
+            if e in copies:
+                copies[e].wait()
+                for later in then.get(e, ()):
+                    later.start()
             one = dot(jnp.where(row == k, both, 0.0).astype(BF16), blocks[e])
             acc = one if acc is None else acc + one
         parts.append(acc[:8] + acc[8:])
     return jnp.concatenate(parts, axis=0)
 
 
-def pick(z, recv_node, counts):
-    hi, lo = split(z)
-    rows = [part[:, v * NODES : (v + 1) * NODES] for part in (hi, lo) for v in range(VARS)]
-    rows = jnp.concatenate(rows, axis=0).astype(BF16)
+def point_masks(recv_node, counts):
     elem = lax.shift_right_logical(recv_node, 6)
     node = jnp.bitwise_and(recv_node, NODES - 1)
     node_hot = (iota((NODES, RPTS), 0) == node).astype(F32).astype(BF16)
-    at_node = dot(rows, node_hot)
-    at_node = at_node[: VARS * E] + at_node[VARS * E :]
     lane = iota((1, RPTS), 1)
     block = lax.shift_right_logical(lane, 7)
     count = jnp.where(
         block == 0, counts[0], jnp.where(block == 1, counts[1], jnp.where(block == 2, counts[2], counts[3]))
     )
     live = jnp.bitwise_and(lane, 127) < count
-    elem = jnp.where(live, elem, -1)
-    elem_hot = iota((E, RPTS), 0) == elem
+    elem_hot = (iota((E, RPTS), 0) == jnp.where(live, elem, -1)).astype(F32)
+    return node_hot, elem_hot
+
+
+def pick(z, masks):
+    node_hot, elem_hot = masks
+    hi, lo = split(z)
+    rows = [part[:, v * NODES : (v + 1) * NODES] for part in (hi, lo) for v in range(VARS)]
+    rows = jnp.concatenate(rows, axis=0).astype(BF16)
+    at_node = dot(rows, node_hot)
+    at_node = at_node[: VARS * E] + at_node[VARS * E :]
     return [
-        jnp.sum(jnp.where(elem_hot, at_node[v * E : (v + 1) * E], 0.0), axis=0, keepdims=True)
+        jnp.sum(at_node[v * E : (v + 1) * E] * elem_hot, axis=0, keepdims=True)
         for v in range(VARS)
     ]
 
@@ -185,53 +207,13 @@
     return jnp.concatenate([out[v * E : (v + 1) * E] for v in range(VARS)], axis=1)
 
 
-def first_kernel(
-    x_hbm, blocks_ref, node_hbm, owner_hbm, elem_hbm, coord_hbm, count_hbm,
-    z_ref, pay_ref, rank_ref,
-    x_ref, node_ref, owner_ref, elem_ref, coord_ref, count_ref, small_sems, buf, sems,
-):
-    small = [
-        pltpu.make_async_copy(src, dst, small_sems.at[i])
-        for i, (src, dst) in enumerate(
-            [
-                (owner_hbm, owner_ref), (x_hbm, x_ref), (node_hbm, node_ref),
-                (elem_hbm, elem_ref), (coord_hbm, coord_ref), (count_hbm, count_ref),
-            ]
-        )
-    ]
-    copies = stream(blocks_ref, buf, sems)
-    for one in small + copies:
-        one.start()
-    for one in small:
-        one.wait()
-    hot = owner_one_hot(owner_ref[...])
-    hot16 = hot.astype(BF16)
-    earlier = (iota((RPTS, RPTS), 0) < iota((RPTS, RPTS), 1)).astype(F32).astype(BF16)
-    rank = jnp.sum(hot * dot(hot16, earlier), axis=0, keepdims=True).astype(jnp.int32)
-    rank_ref[...] = rank
-    z = block_solve(x_ref[...], buf, copies)
-    z_ref[...] = z
-    counts = [count_ref[0, i] for i in range(4)]
-    comps = pick(z, node_ref[...], counts)
-    comps += [coord_ref[c : c + 1, :] for c in range(3)]
-    comps.append(elem_ref[...].astype(F32))
-    pay_ref[...] = pack(hot16, rank, comps)
-
-
-def face_kernel(
-    z_ref, x_ref, jac_ref, nbr_ref, spread_ref,
-    base_ref, first_ref, second_ref, traces, outs, buf, sems,
-):
-    copies = stream(jac_ref, buf, sems)
-    for one in copies:
-        one.start()
-    hi, lo = split(z_ref[...])
-    traces[...] = dot_nt(jnp.concatenate([hi, lo], axis=0).astype(BF16), spread_ref[...])
+def face_traces(z, jac, copies, spread, traces, outs):
+    hi, lo = split(z)
+    traces[...] = dot_nt(jnp.concatenate([hi, lo], axis=0).astype(BF16), spread)
     own_face = iota((16, 6 * FACEW), 1) // FACEW == iota((16, 6 * FACEW), 0) % 8
-    step = E // CHUNKS
     for e in range(E):
-        if e % step == 0:
-            copies[e // step].wait()
+        if e in copies:
+            copies[e].wait()
         both = jnp.concatenate(
             [
                 jnp.broadcast_to(traces[pl.ds(e, 1), :], (8, 6 * FACEW)),
@@ -239,21 +221,65 @@
             ],
             axis=0,
         )
-        one = dot(jnp.where(own_face, both, 0.0).astype(BF16), buf[e])
+        one = dot(jnp.where(own_face, both, 0.0).astype(BF16), jac[e])
         outs[8 * e : 8 * e + 8, 0:FACEW] = one[:8] + one[8:]
-    out = jnp.concatenate(
+    return jnp.concatenate(
         [outs[pl.ds(f, E, stride=8), :][:, :FACEW] for f in range(6)], axis=0
     )
+
+
+def faces(x, z, jac, copies, hots, spread_ref, base_ref, first_ref, second_ref, traces, outs):
+    out = face_traces(z, jac, copies, spread_ref[...], traces, outs)
     hi, lo = split(out)
     hi, lo = hi.astype(BF16), lo.astype(BF16)
-    local_hot, iface_hot = neighbour_one_hots(nbr_ref[...])
+    local_hot, iface_hot = hots
     outgoing = dot(iface_hot, hi) + dot(iface_hot, lo)
     odd = lax.axis_index("dom") % 2 == 1
     low, high = outgoing[:E], outgoing[E:]
     first_ref[...] = jnp.where(odd, low, high)
     second_ref[...] = jnp.where(odd, high, low)
-    incoming = dot_tn(local_hot, hi) + dot_tn(local_hot, lo)
-    base_ref[...] = x_ref[...] - spread_faces(incoming, spread_ref)
+    base_ref[...] = x - spread_faces(dot_tn(local_hot, hi), dot_tn(local_hot, lo), spread_ref)
+
+
+def first_kernel(
+    x_hbm, blocks_hbm, jac_hbm, node_hbm, owner_hbm, elem_hbm, coord_hbm, count_hbm, nbr_hbm, spread_hbm,
+    base_ref, first_ref, second_ref, pay_ref, rank_ref,
+    x_ref, node_ref, owner_ref, elem_ref, coord_ref, count_ref, nbr_ref, spread_ref, small_sems,
+    blocks, block_sems, jac, jac_sems, traces, outs,
+):
+    small = [
+        pltpu.make_async_copy(src, dst, small_sems.at[i])
+        for i, (src, dst) in enumerate(
+            [
+                (owner_hbm, owner_ref), (x_hbm, x_ref), (node_hbm, node_ref), (elem_hbm, elem_ref),
+                (coord_hbm, coord_ref), (count_hbm, count_ref), (nbr_hbm, nbr_ref), (spread_hbm, spread_ref),
+            ]
+        )
+    ]
+    block_copies = stream(blocks_hbm, blocks, block_sems, BLOCK_CHUNKS)
+    jac_copies = stream(jac_hbm, jac, jac_sems, JAC_CHUNKS)
+    for one in small[:2]:
+        one.start()
+    then = start_order(block_copies, jac_copies)
+    for one in small[2:]:
+        one.start()
+    for one in small[:2]:
+        one.wait()
+    hot = owner_one_hot(owner_ref[...])
+    hot16 = hot.astype(BF16)
+    earlier = (iota((RPTS, RPTS), 0) < iota((RPTS, RPTS), 1)).astype(F32).astype(BF16)
+    rank = jnp.sum(hot * dot(hot16, earlier), axis=0, keepdims=True).astype(jnp.int32)
+    rank_ref[...] = rank
+    x = x_ref[...]
+    z = block_solve(x, blocks, block_copies, then)
+    for one in small[2:]:
+        one.wait()
+    masks = point_masks(node_ref[...], [count_ref[0, i] for i in range(4)])
+    comps = pick(z, masks)
+    comps += [coord_ref[c : c + 1, :] for c in range(3)]
+    comps.append(elem_ref[...].astype(F32))
+    pay_ref[...] = pack(hot16, rank, comps)
+    faces(x, z, jac, jac_copies, neighbour_one_hots(nbr_ref[...]), spread_ref, base_ref, first_ref, second_ref, traces, outs)
 
 
 def neighbour_one_hots(nbr):
@@ -268,8 +294,7 @@
     return hot[: 6 * E], hot[6 * E :]
 
 
-def spread_faces(incoming, spread_ref):
-    hi, lo = split(incoming)
+def spread_faces(hi, lo, spread_ref):
     acc = None
     for f in range(6):
         both = jnp.concatenate([hi[f * E : (f + 1) * E], lo[f * E : (f + 1) * E]], axis=0)
@@ -284,8 +309,8 @@
     low, high = jnp.where(odd, first, second), jnp.where(odd, second, first)
     hi, lo = split(jnp.concatenate([low, high], axis=0))
     _, iface_hot = neighbour_one_hots(nbr_ref[...])
-    incoming = dot_tn(iface_hot, hi.astype(BF16)) + dot_tn(iface_hot, lo.astype(BF16))
-    out_ref[...] = base_ref[...] - spread_faces(incoming, spread_ref)
+    hi, lo = dot_tn(iface_hot, hi.astype(BF16)), dot_tn(iface_hot, lo.astype(BF16))
+    out_ref[...] = base_ref[...] - spread_faces(hi, lo, spread_ref)
 
 
 def with_scalars(table, scalars):
@@ -301,23 +326,23 @@
 
 
 def second_kernel(
-    base_ref, got_ref, b_ref, blocks_ref, node_ref, owner_ref, rank_ref, count_ref,
-    u_ref, z_ref, pay_ref, table, buf, sems,
+    base_ref, got_ref, b_ref, blocks_hbm, jac_hbm, node_ref, owner_ref, rank_ref, count_ref, nbr_ref, spread_ref,
+    u_ref, out_ref, first_ref, second_ref, pay_ref,
+    table, blocks, block_sems, jac, jac_sems, traces, outs,
 ):
-    copies = stream(blocks_ref, buf, sems)
-    for one in copies:
-        one.start()
+    block_copies = stream(blocks_hbm, blocks, block_sems, BLOCK_CHUNKS)
+    jac_copies = stream(jac_hbm, jac, jac_sems, JAC_CHUNKS)
+    then = start_order(block_copies, jac_copies)
     got = got_ref[...]
     u = base_ref[...] - interpolate(got, got, table)
     u_ref[...] = u
     b = b_ref[...]
-    z = block_solve(u, buf, copies)
-    z_ref[...] = z
-    counts = [count_ref[0, i] for i in range(4)]
-    comps = pick(z, node_ref[...], counts)
+    scalars = [total(b * b), total(b * u)]
+    z = block_solve(u, blocks, block_copies, then)
+    masks = point_masks(node_ref[...], [count_ref[0, i] for i in range(4)])
     hot = owner_one_hot(owner_ref[...]).astype(BF16)
-    pay = pack(hot, rank_ref[...], comps)
-    pay_ref[...] = with_scalars(pay, [total(b * b), total(b * u)])
+    pay_ref[...] = with_scalars(pack(hot, rank_ref[...], pick(z, masks)), scalars)
+    faces(u, z, jac, jac_copies, neighbour_one_hots(nbr_ref[...]), spread_ref, out_ref, first_ref, second_ref, traces, outs)
 
 
 def third_kernel(base_ref, got_ref, first_ref, b_ref, u_ref, rest_ref, pay_ref, known_ref, table):
@@ -415,60 +440,51 @@
     table = ((PEERS, PEERS), F32)
     half = ((E, FACEW), F32)
     row = pltpu.VMEM((1, RPTS), jnp.int32)
-    block_scratch = [pltpu.VMEM((E, BLOCK, BLOCK), BF16), pltpu.SemaphoreType.DMA((CHUNKS,))]
-    blocks = in_hbm(block_inv)
-    jac = in_hbm(jac)
+    matrices = [
+        pltpu.VMEM((E, BLOCK, BLOCK), BF16), pltpu.SemaphoreType.DMA((len(BLOCK_CHUNKS),)),
+        pltpu.VMEM((E, 6 * FACEW, FACEW), BF16), pltpu.SemaphoreType.DMA((len(JAC_CHUNKS),)),
+    ]
+    face_scratch = [pltpu.VMEM((2 * E, 6 * FACEW), F32), pltpu.VMEM((8 * E, PEERS), F32)]
     rows_scratch = pltpu.VMEM((8 * (13 + 2 * VARS), PEERS), F32)
 
-    def faces(z, x):
-        base, first, second = call(
-            face_kernel,
-            [VM, VM, HBM, VM, VM],
-            [full, half, half],
-            [
-                pltpu.VMEM((2 * E, 6 * FACEW), F32),
-                pltpu.VMEM((8 * E, PEERS), F32),
-                pltpu.VMEM((E, 6 * FACEW, FACEW), BF16),
-                pltpu.SemaphoreType.DMA((CHUNKS,)),
-            ],
-            z, x, jac, nbr, spread,
-        )
+    def arrive(base, first, second):
         second = lax.ppermute(second, "dom", odd_pairs)
         first = lax.ppermute(first, "dom", even_pairs)
         return call(arrived_kernel, [VM] * 5, [full], [], base, first, second, nbr, spread)[0]
 
-    z1, pay1, rank = call(
+    small = (node, owner, elem, donor_coords, recv_counts, nbr, spread)
+    base, first, second, pay, rank = call(
         first_kernel,
-        [HBM] * 7,
-        [full, table, ((1, RPTS), jnp.int32)],
+        [HBM] * 10,
+        [full, half, half, table, ((1, RPTS), jnp.int32)],
         [
             pltpu.VMEM((E, BLOCK), F32), row, row, row, pltpu.VMEM((3, RPTS), F32),
-            pltpu.SMEM((1, 4), jnp.int32),
-            pltpu.SemaphoreType.DMA((6,)),
+            pltpu.SMEM((1, 4), jnp.int32), pltpu.VMEM((6, E), jnp.int32),
+            pltpu.VMEM((6 * FACEW, BLOCK), BF16), pltpu.SemaphoreType.DMA((8,)),
         ]
-        + block_scratch,
-        in_hbm(grad_rhs), blocks, in_hbm(node), in_hbm(owner), in_hbm(elem),
-        in_hbm(donor_coords), in_hbm(recv_counts),
-    )
-    got1 = exchange(pay1)
-    base1 = faces(z1, grad_rhs)
-    u, z2, pay2 = call(
+        + matrices
+        + face_scratch,
+        *[in_hbm(one) for one in (grad_rhs, block_inv, jac) + small],
+    )
+    got1 = exchange(pay)
+    base = arrive(base, first, second)
+    u, base, first, second, pay = call(
         second_kernel,
-        [VM, VM, VM, HBM, VM, VM, VM, SM],
-        [full, full, table],
-        [rows_scratch] + block_scratch,
-        base1, got1, grad_rhs, blocks, node, owner, rank, recv_counts,
-    )
-    got2 = exchange(pay2)
-    base2 = faces(z2, u)
-    rest, pay3, known = call(
+        [VM] * 3 + [HBM] * 2 + [VM] * 3 + [SM, VM, VM],
+        [full, full, half, half, table],
+        [rows_scratch] + matrices + face_scratch,
+        base, got1, grad_rhs, in_hbm(block_inv), in_hbm(jac), node, owner, rank, recv_counts, nbr, spread,
+    )
+    got2 = exchange(pay)
+    base = arrive(base, first, second)
+    rest, pay, known = call(
         third_kernel,
         [VM] * 5,
         [full, table, ((8, PEERS), F32)],
         [rows_scratch],
-        base2, got2, got1, grad_rhs, u,
-    )
-    got3 = exchange(pay3)
+        base, got2, got1, grad_rhs, u,
+    )
+    got3 = exchange(pay)
     return call(last_kernel, [VM] * 4, [full], [], got3, known, grad_rhs, rest)[0]
 
 

time: 76.6 us -> 72 us (0.940)
  waiting for transfers between devices: 5.19 us -> 9.96 us
  Pallas kernels: 21.3 us -> 16.7 us
  blocking collectives: 19.8 us -> 17.4 us
  starting transfers between devices: 29.9 us -> 27.5 us
    all_to_all x2, waiting for transfers between devices: 0.01 us -> 4.73 us  [exchange(): lax.all_to_all(table.reshape(PEERS, 1, PEERS), AXES, split_axis=0, concat...]
    pallas_call x8 -> x6, Pallas kernels: 21.3 us -> 16.7 us  [call(): pl.pallas_call(kernel, in_specs=in_specs, out_specs=[VM] * len(outs), out...]
    all_to_all x1, blocking collectives: 19.8 us -> 17.4 us  [exchange(): lax.all_to_all(table.reshape(PEERS, 1, PEERS), AXES, split_axis=0, concat...]
    all_to_all x2, starting transfers between devices: 22.1 us -> 19.8 us  [exchange(): lax.all_to_all(table.reshape(PEERS, 1, PEERS), AXES, split_axis=0, concat...]
  transfers between devices with their start and end apart: 6 -> 6, of which waited for: 2 -> 4; matrix products, arithmetic and copies ran while one was open for 0% -> 0% of each run, Pallas kernels for 10% -> 1%
where the time goes in v3:
time: 72 us; the launch traced here: 71.8 us
  starting transfers between devices  27.5 us (38%)
  blocking collectives  17.4 us (24%)
  Pallas kernels  16.7 us (23%)
  waiting for transfers between devices  9.96 us (14%)
    all_to_all x2, starting transfers between devices, exchange(): lax.all_to_all(table.reshape(PEERS, 1, PEERS), AXES, split_axis=0, concat...  19.8 us
    all_to_all x1, blocking collectives, exchange(): lax.all_to_all(table.reshape(PEERS, 1, PEERS), AXES, split_axis=0, concat...  17.4 us
    pallas_call x6, Pallas kernels, call(): pl.pallas_call(kernel, in_specs=in_specs, out_specs=[VM] * len(outs), out...  16.7 us
    ppermute x2, starting transfers between devices, arrive(): second = lax.ppermute(second, 'dom', odd_pairs)  5.46 us
    ppermute x2, waiting for transfers between devices, arrive(): second = lax.ppermute(second, 'dom', odd_pairs)  5.23 us
    all_to_all x2, waiting for transfers between devices, exchange(): lax.all_to_all(table.reshape(PEERS, 1, PEERS), AXES, split_axis=0, concat...  4.73 us
    ppermute x2, starting transfers between devices, arrive(): first = lax.ppermute(first, 'dom', even_pairs)  2.29 us
  transfers between devices with their start and end apart: 6, of which 4 were waited for; matrix products, arithmetic and copies ran while one was open for 0% of the time, Pallas kernels for 1%

profile of v3, /device:TPU:1, one launch (start us, length us, event | category | flops | bytes accessed | tf_op | source)
XLA Modules:
  0.0 71.8 jit_solution(5775356948741886273)
XLA Ops:
  0.0 0.0 copy-start
  0.0 0.0 copy-start.1
  0.0 0.0 copy-start.5
  0.0 0.0 copy-start.4
  0.0 0.0 copy-start.3
  0.0 0.0 copy-start.2
  0.0 6.7 %first_kernel.1 = (f32[32,320]{1,0:T(8,128)S(1)}, f32[32,80]{1,0:T(8,128)S(1)}, f32[32,80]{1,0:T(8,128)S(1)}, f32[128,128]{1,0:T(8,128)}, s32[1,512]{1,0:T(1,128)S(1)}) custom-call(f32[32,320]{1,0:T(8,128)} %b_ref.5, bf16[32,320,320]{2,1,0:T(8,128)(2,1)} %blocks_hbm.3, bf16[32,480,80]{2,1,0:T(8,128)(2,1)} %bitcast.30, s32[1,512]{1,0:T(1,128)} %bitcast.26, ...), custom_call_target="tpu_custom_call" | custom-call | tf_op jit(solution)/shard_map/first_kernel/pallas_call | solution.py:410
  6.7 11.5 %all-to-all-start = ((f32[128,1,128]{2,1,0:T(1,128)}), f32[128,1,128]{2,1,0:T(1,128)S(1)}, u32[]{:S(2)}, u32[]{:S(2)}) async-start(f32[128,1,128]{2,1,0:T(1,128)} %bitcast.6), calls=%async_computation | async-start | bytes 131072 | tf_op jit(solution)/shard_map/all_to_all | solution.py:422
  18.2 1.1 %collective-permute-start = (f32[32,80]{1,0:T(8,128)S(1)}, f32[32,80]{1,0:T(8,128)S(1)}, u32[]{:S(2)}, u32[]{:S(2)}) collective-permute-start(f32[32,80]{1,0:T(8,128)S(1)} %get-tuple-element.19), channel_id=1, source_target_pairs={{0,1},{1,0},{2,3},{3,2},{4,5},{5,4},{6,7},{7,6},{8,9},{9,8},{10,11... | collective-permute-start | bytes 30728 | tf_op jit(solution)/shard_map/ppermute | solution.py:452
  19.4 2.7 %collective-permute-start.1 = (f32[32,80]{1,0:T(8,128)S(1)}, f32[32,80]{1,0:T(8,128)S(1)}, u32[]{:S(2)}, u32[]{:S(2)}) collective-permute-start(f32[32,80]{1,0:T(8,128)S(1)} %get-tuple-element.20), channel_id=1, source_target_pairs={{1,2},{2,1},{3,4},{4,3},{5,6},{6,5},{7,8},{8,7},{9,10},{10,9},{11,... | collective-permute-start | bytes 30728 | tf_op jit(solution)/shard_map/ppermute | solution.py:451
  22.1 0.0 collective-permute-done.first_ref
  22.1 2.6 %collective-permute-done.1.second_ref = f32[32,80]{1,0:T(8,128)S(1)} collective-permute-done((f32[32,80]{1,0:T(8,128)S(1)}, f32[32,80]{1,0:T(8,128)S(1)}, u32[]{:S(2)}, u32[]{:S(2)}) %collective-permute-start.1) | collective-permute-done | bytes 10272 | tf_op jit(solution)/shard_map/ppermute | solution.py:451
  24.7 0.0 copy-done
  24.7 0.0 copy-done.2
  24.7 0.5 arrived_kernel.2.base_ref
  25.2 2.4 %all-to-all-done = f32[128,1,128]{2,1,0:T(1,128)S(1)} async-done(((f32[128,1,128]{2,1,0:T(1,128)}), f32[128,1,128]{2,1,0:T(1,128)S(1)}, u32[]{:S(2)}, u32[]{:S(2)}) %all-to-all-start) | async-done | bytes 65568 | tf_op jit(solution)/shard_map/all_to_all | solution.py:422
  27.6 0.0 copy-done.1
  27.6 0.0 copy-done.5
  27.6 0.0 copy-done.4
  27.6 0.0 copy-done.3
  27.6 7.3 %second_kernel.1 = (f32[32,320]{1,0:T(8,128)S(1)}, f32[32,320]{1,0:T(8,128)S(1)}, f32[32,80]{1,0:T(8,128)S(1)}, f32[32,80]{1,0:T(8,128)S(1)}, f32[128,128]{1,0:T(8,128)}) custom-call(f32[32,320]{1,0:T(8,128)S(1)} %arrived_kernel.2.base_ref, f32[128,128]{1,0:T(8,128)S(1)} %bitcast.17, f32[32,320]{1,0:T(8,128)S(1)} %copy-done.1, ...), custom_call_target="tpu_custom_call" | custom-call | tf_op jit(solution)/shard_map/second_kernel/pallas_call | solution.py:410
  34.9 8.2 %all-to-all-start.1 = ((f32[128,1,128]{2,1,0:T(1,128)}), f32[128,1,128]{2,1,0:T(1,128)S(1)}, u32[]{:S(2)}, u32[]{:S(2)}) async-start(f32[128,1,128]{2,1,0:T(1,128)} %bitcast.9), calls=%async_computation.1 | async-start | bytes 131072 | tf_op jit(solution)/shard_map/all_to_all | solution.py:422
  43.2 1.1 %collective-permute-start.2 = (f32[32,80]{1,0:T(8,128)S(1)}, f32[32,80]{1,0:T(8,128)S(1)}, u32[]{:S(2)}, u32[]{:S(2)}) collective-permute-start(f32[32,80]{1,0:T(8,128)S(1)} %get-tuple-element.24), channel_id=1, source_target_pairs={{0,1},{1,0},{2,3},{3,2},{4,5},{5,4},{6,7},{7,6},{8,9},{9,8},{10,11... | collective-permute-start | bytes 30728 | tf_op jit(solution)/shard_map/ppermute | solution.py:452
  44.3 2.7 %collective-permute-start.3 = (f32[32,80]{1,0:T(8,128)S(1)}, f32[32,80]{1,0:T(8,128)S(1)}, u32[]{:S(2)}, u32[]{:S(2)}) collective-permute-start(f32[32,80]{1,0:T(8,128)S(1)} %get-tuple-element.25), channel_id=1, source_target_pairs={{1,2},{2,1},{3,4},{4,3},{5,6},{6,5},{7,8},{8,7},{9,10},{10,9},{11,... | collective-permute-start | bytes 30728 | tf_op jit(solution)/shard_map/ppermute | solution.py:451
  47.1 0.0 collective-permute-done.2.first_ref
  47.1 2.6 %collective-permute-done.3.second_ref = f32[32,80]{1,0:T(8,128)S(1)} collective-permute-done((f32[32,80]{1,0:T(8,128)S(1)}, f32[32,80]{1,0:T(8,128)S(1)}, u32[]{:S(2)}, u32[]{:S(2)}) %collective-permute-start.3) | collective-permute-done | bytes 10272 | tf_op jit(solution)/shard_map/ppermute | solution.py:451
  49.7 0.5 arrived_kernel.3.base_ref
  50.2 2.4 %all-to-all-done.1 = f32[128,1,128]{2,1,0:T(1,128)S(1)} async-done(((f32[128,1,128]{2,1,0:T(1,128)}), f32[128,1,128]{2,1,0:T(1,128)S(1)}, u32[]{:S(2)}, u32[]{:S(2)}) %all-to-all-start.1) | async-done | bytes 65568 | tf_op jit(solution)/shard_map/all_to_all | solution.py:422
  52.5 0.7 %third_kernel.1 = (f32[32,320]{1,0:T(8,128)S(1)}, f32[128,128]{1,0:T(8,128)S(1)}, f32[8,128]{1,0:T(8,128)S(1)}) custom-call(f32[32,320]{1,0:T(8,128)S(1)} %arrived_kernel.3.base_ref, f32[128,128]{1,0:T(8,128)S(1)} %bitcast.19, f32[128,128]{1,0:T(8,128)S(1)} %bitcast.18, f32[32,320]{1,0:T(8,128)S(1)} %copy-done.1, f32[32,320]{1,0:T(8,128)S(1)} %get-tuple-element.27.u_ref), custom_call_target="tpu_custom_call" | custom-call | tf_op jit(solution)/shard_map/third_kernel/pallas_call | solution.py:410
  53.3 17.4 %all_to_all.15 = f32[128,1,128]{2,1,0:T(1,128)S(1)} all-to-all(f32[128,1,128]{2,1,0:T(1,128)S(1)} %bitcast.25), channel_id=1, replica_groups=mesh['grp'=4,'dom'=32] {'grp','dom'}, dimensions={0} | all-to-all | bytes 131072 | tf_op jit(solution)/shard_map/all_to_all | solution.py:422
  70.7 1.1 %last_kernel.1 = f32[32,320]{1,0:T(8,128)} custom-call(f32[128,128]{1,0:T(8,128)S(1)} %bitcast.20, f32[8,128]{1,0:T(8,128)S(1)} %get-tuple-element.29.known_ref, f32[32,320]{1,0:T(8,128)S(1)} %copy-done.1, f32[32,320]{1,0:T(8,128)S(1)} %get-tuple-element.30.rest_ref), custom_call_target="tpu_custom_call" | custom-call | tf_op jit(solution)/shard_map/last_kernel/pallas_call | solution.py:410
Async XLA Ops:
  0.0 24.7 %copy-start = (bf16[480,320]{1,0:T(8,128)(2,1)S(1)}, bf16[480,320]{1,0:T(8,128)(2,1)}, u32[]{:S(2)}) copy-start(bf16[480,320]{1,0:T(8,128)(2,1)} %constant.2.clone.spread_hbm.spread_ref) | copy-start | bytes 921604
  0.0 27.6 %copy-start.1 = (f32[32,320]{1,0:T(8,128)S(1)}, f32[32,320]{1,0:T(8,128)}, u32[]{:S(2)}) copy-start(f32[32,320]{1,0:T(8,128)} %b_ref.5) | copy-start | bytes 122884
  0.0 27.6 %copy-start.5 = (s32[1,4]{1,0:T(1,128)S(1)}, s32[1,4]{1,0:T(1,128)}, u32[]{:S(2)}) copy-start(s32[1,4]{1,0:T(1,128)} %count_ref.1) | copy-start | bytes 52
  0.0 27.6 %copy-start.4 = (s32[512,1]{0,1:T(1,128)S(1)}, s32[512,1]{0,1:T(1,128)}, u32[]{:S(2)}) copy-start(s32[512,1]{0,1:T(1,128)} %param.15) | copy-start | bytes 6148
  0.0 27.6 %copy-start.3 = (s32[512]{0:T(512)S(1)}, s32[512]{0:T(512)}, u32[]{:S(2)}) copy-start(s32[512]{0:T(512)} %param.14) | copy-start | bytes 6148
  0.0 24.7 %copy-start.2 = (s32[32,6]{0,1:T(8,128)S(1)}, s32[32,6]{0,1:T(8,128)}, u32[]{:S(2)}) copy-start(s32[32,6]{0,1:T(8,128)} %param.13) | copy-start | bytes 2308
  6.7 20.9 %all-to-all-start = ((f32[128,1,128]{2,1,0:T(1,128)}), f32[128,1,128]{2,1,0:T(1,128)S(1)}, u32[]{:S(2)}, u32[]{:S(2)}) async-start(f32[128,1,128]{2,1,0:T(1,128)} %bitcast.6), calls=%async_computation | async-start | bytes 131072 | tf_op jit(solution)/shard_map/all_to_all | solution.py:422
  18.2 3.9 %collective-permute-start = (f32[32,80]{1,0:T(8,128)S(1)}, f32[32,80]{1,0:T(8,128)S(1)}, u32[]{:S(2)}, u32[]{:S(2)}) collective-permute-start(f32[32,80]{1,0:T(8,128)S(1)} %get-tuple-element.19), channel_id=1, source_target_pairs={{0,1},{1,0},{2,3},{3,2},{4,5},{5,4},{6,7},{7,6},{8,9},{9,8},{10,11... | collective-permute-start | bytes 30728 | tf_op jit(solution)/shard_map/ppermute | solution.py:452
  19.4 5.4 %collective-permute-start.1 = (f32[32,80]{1,0:T(8,128)S(1)}, f32[32,80]{1,0:T(8,128)S(1)}, u32[]{:S(2)}, u32[]{:S(2)}) collective-permute-start(f32[32,80]{1,0:T(8,128)S(1)} %get-tuple-element.20), channel_id=1, source_target_pairs={{1,2},{2,1},{3,4},{4,3},{5,6},{6,5},{7,8},{8,7},{9,10},{10,9},{11,... | collective-permute-start | bytes 30728 | tf_op jit(solution)/shard_map/ppermute | solution.py:451
  34.9 17.6 %all-to-all-start.1 = ((f32[128,1,128]{2,1,0:T(1,128)}), f32[128,1,128]{2,1,0:T(1,128)S(1)}, u32[]{:S(2)}, u32[]{:S(2)}) async-start(f32[128,1,128]{2,1,0:T(1,128)} %bitcast.9), calls=%async_computation.1 | async-start | bytes 131072 | tf_op jit(solution)/shard_map/all_to_all | solution.py:422
  43.2 3.9 %collective-permute-start.2 = (f32[32,80]{1,0:T(8,128)S(1)}, f32[32,80]{1,0:T(8,128)S(1)}, u32[]{:S(2)}, u32[]{:S(2)}) collective-permute-start(f32[32,80]{1,0:T(8,128)S(1)} %get-tuple-element.24), channel_id=1, source_target_pairs={{0,1},{1,0},{2,3},{3,2},{4,5},{5,4},{6,7},{7,6},{8,9},{9,8},{10,11... | collective-permute-start | bytes 30728 | tf_op jit(solution)/shard_map/ppermute | solution.py:452
  44.3 5.4 %collective-permute-start.3 = (f32[32,80]{1,0:T(8,128)S(1)}, f32[32,80]{1,0:T(8,128)S(1)}, u32[]{:S(2)}, u32[]{:S(2)}) collective-permute-start(f32[32,80]{1,0:T(8,128)S(1)} %get-tuple-element.25), channel_id=1, source_target_pairs={{1,2},{2,1},{3,4},{4,3},{5,6},{6,5},{7,8},{8,7},{9,10},{10,9},{11,... | collective-permute-start | bytes 30728 | tf_op jit(solution)/shard_map/ppermute | solution.py:451

commit v4 on v3

--- a/solution.py
+++ b/solution.py
@@ -303,14 +303,27 @@
     return acc[:E] + acc[E:]
 
 
-def arrived_kernel(base_ref, first_ref, second_ref, nbr_ref, spread_ref, out_ref):
+def arrived(first, second, nbr, spread_ref):
     odd = lax.axis_index("dom") % 2 == 1
-    first, second = first_ref[...], second_ref[...]
     low, high = jnp.where(odd, first, second), jnp.where(odd, second, first)
     hi, lo = split(jnp.concatenate([low, high], axis=0))
-    _, iface_hot = neighbour_one_hots(nbr_ref[...])
+    _, iface_hot = neighbour_one_hots(nbr)
     hi, lo = dot_tn(iface_hot, hi.astype(BF16)), dot_tn(iface_hot, lo.astype(BF16))
-    out_ref[...] = base_ref[...] - spread_faces(hi, lo, spread_ref)
+    return spread_faces(hi, lo, spread_ref)
+
+
+def late_interp_kernel(got_ref, first_ref, out_ref, table):
+    out_ref[...] = interpolate(got_ref[...], first_ref[...], table)
+
+
+def interp_kernel(got_ref, blocks_hbm, interp_ref, blocks_ref, table, sems):
+    copies = list(stream(blocks_hbm, blocks_ref, sems, BLOCK_CHUNKS).values())
+    for one in copies:
+        one.start()
+    got = got_ref[...]
+    interp_ref[...] = interpolate(got, got, table)
+    for one in copies:
+        one.wait()
 
 
 def with_scalars(table, scalars):
@@ -326,29 +339,33 @@
 
 
 def second_kernel(
-    base_ref, got_ref, b_ref, blocks_hbm, jac_hbm, node_ref, owner_ref, rank_ref, count_ref, nbr_ref, spread_ref,
+    base_ref, first_in, second_in, interp_ref, b_ref, blocks_ref, jac_hbm,
+    node_ref, owner_ref, rank_ref, count_ref, nbr_ref, spread_ref,
     u_ref, out_ref, first_ref, second_ref, pay_ref,
-    table, blocks, block_sems, jac, jac_sems, traces, outs,
+    jac, jac_sems, traces, outs,
 ):
-    block_copies = stream(blocks_hbm, blocks, block_sems, BLOCK_CHUNKS)
     jac_copies = stream(jac_hbm, jac, jac_sems, JAC_CHUNKS)
-    then = start_order(block_copies, jac_copies)
-    got = got_ref[...]
-    u = base_ref[...] - interpolate(got, got, table)
+    for one in jac_copies.values():
+        one.start()
+    b = b_ref[...]
+    nbr = nbr_ref[...]
+    u = base_ref[...] - interp_ref[...] - arrived(first_in[...], second_in[...], nbr, spread_ref)
     u_ref[...] = u
-    b = b_ref[...]
     scalars = [total(b * b), total(b * u)]
-    z = block_solve(u, blocks, block_copies, then)
+    z = block_solve(u, blocks_ref, {}, {})
     masks = point_masks(node_ref[...], [count_ref[0, i] for i in range(4)])
     hot = owner_one_hot(owner_ref[...]).astype(BF16)
     pay_ref[...] = with_scalars(pack(hot, rank_ref[...], pick(z, masks)), scalars)
-    faces(u, z, jac, jac_copies, neighbour_one_hots(nbr_ref[...]), spread_ref, out_ref, first_ref, second_ref, traces, outs)
-
-
-def third_kernel(base_ref, got_ref, first_ref, b_ref, u_ref, rest_ref, pay_ref, known_ref, table):
-    got = got_ref[...]
-    w = base_ref[...] - interpolate(got, first_ref[...], table)
-    bb, bu = read_scalars(got, 2)
+    faces(u, z, jac, jac_copies, neighbour_one_hots(nbr), spread_ref, out_ref, first_ref, second_ref, traces, outs)
+
+
+def third_kernel(
+    base_ref, first_ref, second_ref, nbr_ref, spread_ref, interp_ref, got_ref, b_ref, u_ref,
+    rest_ref, pay_ref, known_ref,
+):
+    late = arrived(first_ref[...], second_ref[...], nbr_ref[...], spread_ref)
+    w = base_ref[...] - interp_ref[...] - late
+    bb, bu = read_scalars(got_ref[...], 2)
     h00 = bu / (bb + EPS)
     b = b_ref[...]
     u = u_ref[...]
@@ -447,10 +464,8 @@
     face_scratch = [pltpu.VMEM((2 * E, 6 * FACEW), F32), pltpu.VMEM((8 * E, PEERS), F32)]
     rows_scratch = pltpu.VMEM((8 * (13 + 2 * VARS), PEERS), F32)
 
-    def arrive(base, first, second):
-        second = lax.ppermute(second, "dom", odd_pairs)
-        first = lax.ppermute(first, "dom", even_pairs)
-        return call(arrived_kernel, [VM] * 5, [full], [], base, first, second, nbr, spread)[0]
+    def swap(first, second):
+        return lax.ppermute(first, "dom", even_pairs), lax.ppermute(second, "dom", odd_pairs)
 
     small = (node, owner, elem, donor_coords, recv_counts, nbr, spread)
     base, first, second, pay, rank = call(
@@ -467,22 +482,30 @@
         *[in_hbm(one) for one in (grad_rhs, block_inv, jac) + small],
     )
     got1 = exchange(pay)
-    base = arrive(base, first, second)
+    first, second = swap(first, second)
+    interp, blocks = call(
+        interp_kernel,
+        [VM, HBM],
+        [full, ((E, BLOCK, BLOCK), BF16)],
+        [rows_scratch, matrices[1]],
+        got1, in_hbm(block_inv),
+    )
     u, base, first, second, pay = call(
         second_kernel,
-        [VM] * 3 + [HBM] * 2 + [VM] * 3 + [SM, VM, VM],
+        [VM] * 6 + [HBM] + [VM] * 3 + [SM, VM, VM],
         [full, full, half, half, table],
-        [rows_scratch] + matrices + face_scratch,
-        base, got1, grad_rhs, in_hbm(block_inv), in_hbm(jac), node, owner, rank, recv_counts, nbr, spread,
+        matrices[2:] + face_scratch,
+        base, first, second, interp, grad_rhs, blocks, in_hbm(jac), node, owner, rank, recv_counts, nbr, spread,
     )
     got2 = exchange(pay)
-    base = arrive(base, first, second)
+    first, second = swap(first, second)
+    interp = call(late_interp_kernel, [VM, VM], [full], [rows_scratch], got2, got1)[0]
     rest, pay, known = call(
         third_kernel,
-        [VM] * 5,
+        [VM] * 9,
         [full, table, ((8, PEERS), F32)],
-        [rows_scratch],
-        base, got2, got1, grad_rhs, u,
+        [],
+        base, first, second, nbr, spread, interp, got2, grad_rhs, u,
     )
     got3 = exchange(pay)
     return call(last_kernel, [VM] * 4, [full], [], got3, known, grad_rhs, rest)[0]

time: 72 us -> 68.9 us (0.957)
  starting transfers between devices: 27.5 us -> 23.9 us
  waiting for transfers between devices: 9.96 us -> 11.1 us
  blocking collectives: 17.4 us -> 16.3 us
    all_to_all x2, waiting for transfers between devices: 4.73 us -> 11 us  [exchange(): lax.all_to_all(table.reshape(PEERS, 1, PEERS), AXES, split_axis=0, concat...]
    ppermute x4, waiting for transfers between devices: 5.23 us -> 0.01 us  [the longest x2 0.01 us: swap(): lax.ppermute(first, 'dom', even_pairs)]
    all_to_all x2, starting transfers between devices: 19.8 us -> 16.1 us  [exchange(): lax.all_to_all(table.reshape(PEERS, 1, PEERS), AXES, split_axis=0, concat...]
    all_to_all x1, blocking collectives: 17.4 us -> 16.3 us  [exchange(): lax.all_to_all(table.reshape(PEERS, 1, PEERS), AXES, split_axis=0, concat...]
  transfers between devices with their start and end apart: 6 -> 6, of which waited for: 4 -> 2; matrix products, arithmetic and copies ran while one was open for 0% -> 0% of each run, Pallas kernels for 1% -> 6%
where the time goes in v4:
time: 68.9 us; the launch traced here: 68.7 us
  starting transfers between devices  23.9 us (35%)
  Pallas kernels  17.3 us (25%)
  blocking collectives  16.3 us (24%)
  waiting for transfers between devices  11.1 us (16%)
    pallas_call x6, Pallas kernels, call(): pl.pallas_call(kernel, in_specs=in_specs, out_specs=[VM] * len(outs), out...  17.3 us
    all_to_all x1, blocking collectives, exchange(): lax.all_to_all(table.reshape(PEERS, 1, PEERS), AXES, split_axis=0, concat...  16.3 us
    all_to_all x2, starting transfers between devices, exchange(): lax.all_to_all(table.reshape(PEERS, 1, PEERS), AXES, split_axis=0, concat...  16.1 us
    all_to_all x2, waiting for transfers between devices, exchange(): lax.all_to_all(table.reshape(PEERS, 1, PEERS), AXES, split_axis=0, concat...  11 us
    ppermute x2, starting transfers between devices, swap(): lax.ppermute(second, 'dom', odd_pairs)  5.46 us
    ppermute x2, starting transfers between devices, swap(): lax.ppermute(first, 'dom', even_pairs)  2.32 us
  transfers between devices with their start and end apart: 6, of which 2 were waited for; matrix products, arithmetic and copies ran while one was open for 0% of the time, Pallas kernels for 6%

profile of v4, /device:TPU:1, one launch (start us, length us, event | category | flops | bytes accessed | tf_op | source)
XLA Modules:
  0.0 68.7 jit_solution(908672452533160058)
XLA Ops:
  0.0 0.0 copy-start
  0.0 0.0 copy-start.1
  0.0 0.0 copy-start.2
  0.0 0.0 copy-start.3
  0.0 0.0 copy-start.4
  0.0 0.0 copy-start.5
  0.0 6.7 %first_kernel.1 = (f32[32,320]{1,0:T(8,128)S(1)}, f32[32,80]{1,0:T(8,128)S(1)}, f32[32,80]{1,0:T(8,128)S(1)}, f32[128,128]{1,0:T(8,128)}, s32[1,512]{1,0:T(1,128)S(1)}) custom-call(f32[32,320]{1,0:T(8,128)} %b_ref.5, bf16[32,320,320]{2,1,0:T(8,128)(2,1)} %blocks_hbm.3, bf16[32,480,80]{2,1,0:T(8,128)(2,1)} %bitcast.30, s32[1,512]{1,0:T(1,128)} %bitcast.26, ...), custom_call_target="tpu_custom_call" | custom-call | tf_op jit(solution)/shard_map/first_kernel/pallas_call | solution.py:427
  6.7 11.5 %all-to-all-start = ((f32[128,1,128]{2,1,0:T(1,128)}), f32[128,1,128]{2,1,0:T(1,128)S(1)}, u32[]{:S(2)}, u32[]{:S(2)}) async-start(f32[128,1,128]{2,1,0:T(1,128)} %bitcast.6), calls=%async_computation | async-start | bytes 131072 | tf_op jit(solution)/shard_map/all_to_all | solution.py:439
  18.2 1.1 %collective-permute-start = (f32[32,80]{1,0:T(8,128)S(1)}, f32[32,80]{1,0:T(8,128)S(1)}, u32[]{:S(2)}, u32[]{:S(2)}) collective-permute-start(f32[32,80]{1,0:T(8,128)S(1)} %get-tuple-element.21), channel_id=1, source_target_pairs={{0,1},{1,0},{2,3},{3,2},{4,5},{5,4},{6,7},{7,6},{8,9},{9,8},{10,11... | collective-permute-start | bytes 30728 | tf_op jit(solution)/shard_map/ppermute | solution.py:468
  19.4 2.7 %collective-permute-start.1 = (f32[32,80]{1,0:T(8,128)S(1)}, f32[32,80]{1,0:T(8,128)S(1)}, u32[]{:S(2)}, u32[]{:S(2)}) collective-permute-start(f32[32,80]{1,0:T(8,128)S(1)} %get-tuple-element.22), channel_id=1, source_target_pairs={{1,2},{2,1},{3,4},{4,3},{5,6},{6,5},{7,8},{8,7},{9,10},{10,9},{11,... | collective-permute-start | bytes 30728 | tf_op jit(solution)/shard_map/ppermute | solution.py:468
  22.1 5.5 %all-to-all-done = f32[128,1,128]{2,1,0:T(1,128)S(1)} async-done(((f32[128,1,128]{2,1,0:T(1,128)}), f32[128,1,128]{2,1,0:T(1,128)S(1)}, u32[]{:S(2)}, u32[]{:S(2)}) %all-to-all-start) | async-done | bytes 65568 | tf_op jit(solution)/shard_map/all_to_all | solution.py:439
  27.6 3.3 %interp_kernel.1 = (f32[32,320]{1,0:T(8,128)S(1)}, bf16[32,320,320]{2,1,0:T(8,128)(2,1)S(1)}) custom-call(f32[128,128]{1,0:T(8,128)S(1)} %bitcast.17, bf16[32,320,320]{2,1,0:T(8,128)(2,1)} %blocks_hbm.3), custom_call_target="tpu_custom_call" | custom-call | tf_op jit(solution)/shard_map/interp_kernel/pallas_call | solution.py:427
  31.0 0.0 collective-permute-done.first_in
  31.0 0.0 collective-permute-done.1.second_in
  31.0 0.0 copy-done
  31.0 0.0 copy-done.1
  31.0 0.0 copy-done.2
  31.0 0.0 copy-done.3
  31.0 0.0 copy-done.4
  31.0 0.0 copy-done.5
  31.0 5.0 %second_kernel.1 = (f32[32,320]{1,0:T(8,128)S(1)}, f32[32,320]{1,0:T(8,128)S(1)}, f32[32,80]{1,0:T(8,128)S(1)}, f32[32,80]{1,0:T(8,128)S(1)}, f32[128,128]{1,0:T(8,128)}) custom-call(f32[32,320]{1,0:T(8,128)S(1)} %get-tuple-element.20.base_ref, f32[32,80]{1,0:T(8,128)S(1)} %collective-permute-done.first_in, f32[32,80]{1,0:T(8,128)S(1)} %collective-permute-done.1.second_in, ...), custom_call_target="tpu_custom_call" | custom-call | tf_op jit(solution)/shard_map/second_kernel/pallas_call | solution.py:427
  36.0 4.6 %all-to-all-start.1 = ((f32[128,1,128]{2,1,0:T(1,128)}), f32[128,1,128]{2,1,0:T(1,128)S(1)}, u32[]{:S(2)}, u32[]{:S(2)}) async-start(f32[128,1,128]{2,1,0:T(1,128)} %bitcast.9), calls=%async_computation.1 | async-start | bytes 131072 | tf_op jit(solution)/shard_map/all_to_all | solution.py:439
  40.7 1.2 %collective-permute-start.2 = (f32[32,80]{1,0:T(8,128)S(1)}, f32[32,80]{1,0:T(8,128)S(1)}, u32[]{:S(2)}, u32[]{:S(2)}) collective-permute-start(f32[32,80]{1,0:T(8,128)S(1)} %get-tuple-element.28), channel_id=1, source_target_pairs={{0,1},{1,0},{2,3},{3,2},{4,5},{5,4},{6,7},{7,6},{8,9},{9,8},{10,11... | collective-permute-start | bytes 30728 | tf_op jit(solution)/shard_map/ppermute | solution.py:468
  41.8 2.7 %collective-permute-start.3 = (f32[32,80]{1,0:T(8,128)S(1)}, f32[32,80]{1,0:T(8,128)S(1)}, u32[]{:S(2)}, u32[]{:S(2)}) collective-permute-start(f32[32,80]{1,0:T(8,128)S(1)} %get-tuple-element.29), channel_id=1, source_target_pairs={{1,2},{2,1},{3,4},{4,3},{5,6},{6,5},{7,8},{8,7},{9,10},{10,9},{11,... | collective-permute-start | bytes 30728 | tf_op jit(solution)/shard_map/ppermute | solution.py:468
  44.6 5.5 %all-to-all-done.1 = f32[128,1,128]{2,1,0:T(1,128)S(1)} async-done(((f32[128,1,128]{2,1,0:T(1,128)}), f32[128,1,128]{2,1,0:T(1,128)S(1)}, u32[]{:S(2)}, u32[]{:S(2)}) %all-to-all-start.1) | async-done | bytes 65568 | tf_op jit(solution)/shard_map/all_to_all | solution.py:439
  50.1 0.6 late_interp_kernel.1.interp_ref
  50.7 0.0 collective-permute-done.2.first_ref
  50.7 0.0 collective-permute-done.3.second_ref
  50.7 0.6 third_kernel.1
  51.3 16.3 %all_to_all.15 = f32[128,1,128]{2,1,0:T(1,128)S(1)} all-to-all(f32[128,1,128]{2,1,0:T(1,128)S(1)} %bitcast.22), channel_id=1, replica_groups=mesh['grp'=4,'dom'=32] {'grp','dom'}, dimensions={0} | all-to-all | bytes 131072 | tf_op jit(solution)/shard_map/all_to_all | solution.py:439
  67.6 1.1 %last_kernel.1 = f32[32,320]{1,0:T(8,128)} custom-call(f32[128,128]{1,0:T(8,128)S(1)} %bitcast.21, f32[8,128]{1,0:T(8,128)S(1)} %get-tuple-element.33.known_ref, f32[32,320]{1,0:T(8,128)S(1)} %copy-done.1, f32[32,320]{1,0:T(8,128)S(1)} %get-tuple-element.34.rest_ref), custom_call_target="tpu_custom_call" | custom-call | tf_op jit(solution)/shard_map/last_kernel/pallas_call | solution.py:427
Async XLA Ops:
  0.0 31.0 %copy-start = (bf16[480,320]{1,0:T(8,128)(2,1)S(1)}, bf16[480,320]{1,0:T(8,128)(2,1)}, u32[]{:S(2)}) copy-start(bf16[480,320]{1,0:T(8,128)(2,1)} %constant.2.clone.spread_hbm.spread_ref) | copy-start | bytes 921604
  0.0 31.0 %copy-start.1 = (f32[32,320]{1,0:T(8,128)S(1)}, f32[32,320]{1,0:T(8,128)}, u32[]{:S(2)}) copy-start(f32[32,320]{1,0:T(8,128)} %b_ref.5) | copy-start | bytes 122884
  0.0 31.0 %copy-start.2 = (s32[32,6]{0,1:T(8,128)S(1)}, s32[32,6]{0,1:T(8,128)}, u32[]{:S(2)}) copy-start(s32[32,6]{0,1:T(8,128)} %param.13) | copy-start | bytes 2308
  0.0 31.0 %copy-start.3 = (s32[512]{0:T(512)S(1)}, s32[512]{0:T(512)}, u32[]{:S(2)}) copy-start(s32[512]{0:T(512)} %param.14) | copy-start | bytes 6148
  0.0 31.0 %copy-start.4 = (s32[512,1]{0,1:T(1,128)S(1)}, s32[512,1]{0,1:T(1,128)}, u32[]{:S(2)}) copy-start(s32[512,1]{0,1:T(1,128)} %param.15) | copy-start | bytes 6148
  0.0 31.0 %copy-start.5 = (s32[1,4]{1,0:T(1,128)S(1)}, s32[1,4]{1,0:T(1,128)}, u32[]{:S(2)}) copy-start(s32[1,4]{1,0:T(1,128)} %count_ref.1) | copy-start | bytes 52
  6.7 20.9 %all-to-all-start = ((f32[128,1,128]{2,1,0:T(1,128)}), f32[128,1,128]{2,1,0:T(1,128)S(1)}, u32[]{:S(2)}, u32[]{:S(2)}) async-start(f32[128,1,128]{2,1,0:T(1,128)} %bitcast.6), calls=%async_computation | async-start | bytes 131072 | tf_op jit(solution)/shard_map/all_to_all | solution.py:439
  18.2 12.7 %collective-permute-start = (f32[32,80]{1,0:T(8,128)S(1)}, f32[32,80]{1,0:T(8,128)S(1)}, u32[]{:S(2)}, u32[]{:S(2)}) collective-permute-start(f32[32,80]{1,0:T(8,128)S(1)} %get-tuple-element.21), channel_id=1, source_target_pairs={{0,1},{1,0},{2,3},{3,2},{4,5},{5,4},{6,7},{7,6},{8,9},{9,8},{10,11... | collective-permute-start | bytes 30728 | tf_op jit(solution)/shard_map/ppermute | solution.py:468
  19.4 11.6 %collective-permute-start.1 = (f32[32,80]{1,0:T(8,128)S(1)}, f32[32,80]{1,0:T(8,128)S(1)}, u32[]{:S(2)}, u32[]{:S(2)}) collective-permute-start(f32[32,80]{1,0:T(8,128)S(1)} %get-tuple-element.22), channel_id=1, source_target_pairs={{1,2},{2,1},{3,4},{4,3},{5,6},{6,5},{7,8},{8,7},{9,10},{10,9},{11,... | collective-permute-start | bytes 30728 | tf_op jit(solution)/shard_map/ppermute | solution.py:468
  36.0 14.0 %all-to-all-start.1 = ((f32[128,1,128]{2,1,0:T(1,128)}), f32[128,1,128]{2,1,0:T(1,128)S(1)}, u32[]{:S(2)}, u32[]{:S(2)}) async-start(f32[128,1,128]{2,1,0:T(1,128)} %bitcast.9), calls=%async_computation.1 | async-start | bytes 131072 | tf_op jit(solution)/shard_map/all_to_all | solution.py:439
  40.7 10.1 %collective-permute-start.2 = (f32[32,80]{1,0:T(8,128)S(1)}, f32[32,80]{1,0:T(8,128)S(1)}, u32[]{:S(2)}, u32[]{:S(2)}) collective-permute-start(f32[32,80]{1,0:T(8,128)S(1)} %get-tuple-element.28), channel_id=1, source_target_pairs={{0,1},{1,0},{2,3},{3,2},{4,5},{5,4},{6,7},{7,6},{8,9},{9,8},{10,11... | collective-permute-start | bytes 30728 | tf_op jit(solution)/shard_map/ppermute | solution.py:468
  41.8 8.9 %collective-permute-start.3 = (f32[32,80]{1,0:T(8,128)S(1)}, f32[32,80]{1,0:T(8,128)S(1)}, u32[]{:S(2)}, u32[]{:S(2)}) collective-permute-start(f32[32,80]{1,0:T(8,128)S(1)} %get-tuple-element.29), channel_id=1, source_target_pairs={{1,2},{2,1},{3,4},{4,3},{5,6},{6,5},{7,8},{8,7},{9,10},{10,9},{11,... | collective-permute-start | bytes 30728 | tf_op jit(solution)/shard_map/ppermute | solution.py:468

commit v5 on v4

--- a/solution.py
+++ b/solution.py
@@ -15,9 +15,10 @@
 PEERS = 128
 CAP = 8
 RPTS = 512
-BLOCK_CHUNKS = (16, 16)
+BLOCK_CHUNKS = (8, 8, 16)
+KEPT = 8
 START_JAC = 0
-AHEAD = 2
+AHEAD = 3
 JAC_CHUNKS = (16, 16)
 SCALAR_LANE = 96
 GLL = (-1.0, -0.4472135954999579, 0.4472135954999579, 1.0)
@@ -74,6 +75,28 @@
         copies[at] = pltpu.make_async_copy(src.at[pl.ds(at, size)], dst.at[pl.ds(at, size)], sems.at[c])
         at += size
     return copies
+
+
+def stream_blocks(src, kept, rest, sems):
+    copies = {}
+    at = 0
+    for c, size in enumerate(BLOCK_CHUNKS):
+        if at >= KEPT:
+            copies[at] = pltpu.make_async_copy(
+                src.at[pl.ds(at, size)], rest.at[pl.ds(at - KEPT, size)], sems.at[c]
+            )
+        elif kept is not None:
+            copies[at] = pltpu.make_async_copy(src.at[pl.ds(at, size)], kept.at[pl.ds(at, size)], sems.at[c])
+        at += size
+    return copies
+
+
+class Joined:
+    def __init__(self, kept, rest):
+        self.kept, self.rest = kept, rest
+
+    def __getitem__(self, e):
+        return self.kept[e] if e < KEPT else self.rest[e - KEPT]
 
 
 def start_order(blocks, jac):
@@ -236,14 +259,14 @@
     outgoing = dot(iface_hot, hi) + dot(iface_hot, lo)
     odd = lax.axis_index("dom") % 2 == 1
     low, high = outgoing[:E], outgoing[E:]
-    first_ref[...] = jnp.where(odd, low, high)
-    second_ref[...] = jnp.where(odd, high, low)
+    first_ref[...] = jnp.where(odd, high, low)
+    second_ref[...] = jnp.where(odd, low, high)
     base_ref[...] = x - spread_faces(dot_tn(local_hot, hi), dot_tn(local_hot, lo), spread_ref)
 
 
 def first_kernel(
     x_hbm, blocks_hbm, jac_hbm, node_hbm, owner_hbm, elem_hbm, coord_hbm, count_hbm, nbr_hbm, spread_hbm,
-    base_ref, first_ref, second_ref, pay_ref, rank_ref,
+    base_ref, first_ref, second_ref, pay_ref, rank_ref, kept_ref,
     x_ref, node_ref, owner_ref, elem_ref, coord_ref, count_ref, nbr_ref, spread_ref, small_sems,
     blocks, block_sems, jac, jac_sems, traces, outs,
 ):
@@ -256,7 +279,7 @@
             ]
         )
     ]
-    block_copies = stream(blocks_hbm, blocks, block_sems, BLOCK_CHUNKS)
+    block_copies = stream_blocks(blocks_hbm, kept_ref, blocks, block_sems)
     jac_copies = stream(jac_hbm, jac, jac_sems, JAC_CHUNKS)
     for one in small[:2]:
         one.start()
@@ -271,7 +294,7 @@
     rank = jnp.sum(hot * dot(hot16, earlier), axis=0, keepdims=True).astype(jnp.int32)
     rank_ref[...] = rank
     x = x_ref[...]
-    z = block_solve(x, blocks, block_copies, then)
+    z = block_solve(x, Joined(kept_ref, blocks), block_copies, then)
     for one in small[2:]:
         one.wait()
     masks = point_masks(node_ref[...], [count_ref[0, i] for i in range(4)])
@@ -305,7 +328,7 @@
 
 def arrived(first, second, nbr, spread_ref):
     odd = lax.axis_index("dom") % 2 == 1
-    low, high = jnp.where(odd, first, second), jnp.where(odd, second, first)
+    low, high = jnp.where(odd, second, first), jnp.where(odd, first, second)
     hi, lo = split(jnp.concatenate([low, high], axis=0))
     _, iface_hot = neighbour_one_hots(nbr)
     hi, lo = dot_tn(iface_hot, hi.astype(BF16)), dot_tn(iface_hot, lo.astype(BF16))
@@ -317,7 +340,7 @@
 
 
 def interp_kernel(got_ref, blocks_hbm, interp_ref, blocks_ref, table, sems):
-    copies = list(stream(blocks_hbm, blocks_ref, sems, BLOCK_CHUNKS).values())
+    copies = list(stream_blocks(blocks_hbm, None, blocks_ref, sems).values())
     for one in copies:
         one.start()
     got = got_ref[...]
@@ -339,12 +362,12 @@
 
 
 def second_kernel(
-    base_ref, first_in, second_in, interp_ref, b_ref, blocks_ref, jac_hbm,
+    base_ref, first_in, second_in, interp_ref, b_ref, kept_ref, blocks_ref, jac_hbm,
     node_ref, owner_ref, rank_ref, count_ref, nbr_ref, spread_ref,
     u_ref, out_ref, first_ref, second_ref, pay_ref,
     jac, jac_sems, traces, outs,
 ):
-    jac_copies = stream(jac_hbm, jac, jac_sems, JAC_CHUNKS)
+    jac_copies = stream(jac_hbm, jac, jac_sems, (16, 16))
     for one in jac_copies.values():
         one.start()
     b = b_ref[...]
@@ -352,10 +375,12 @@
     u = base_ref[...] - interp_ref[...] - arrived(first_in[...], second_in[...], nbr, spread_ref)
     u_ref[...] = u
     scalars = [total(b * b), total(b * u)]
-    z = block_solve(u, blocks_ref, {}, {})
+    z = block_solve(u, Joined(kept_ref, blocks_ref), {}, {})
+    jac_copies.pop(0).wait()
     masks = point_masks(node_ref[...], [count_ref[0, i] for i in range(4)])
     hot = owner_one_hot(owner_ref[...]).astype(BF16)
     pay_ref[...] = with_scalars(pack(hot, rank_ref[...], pick(z, masks)), scalars)
+    jac_copies.pop(16).wait()
     faces(u, z, jac, jac_copies, neighbour_one_hots(nbr), spread_ref, out_ref, first_ref, second_ref, traces, outs)
 
 
@@ -458,20 +483,20 @@
     half = ((E, FACEW), F32)
     row = pltpu.VMEM((1, RPTS), jnp.int32)
     matrices = [
-        pltpu.VMEM((E, BLOCK, BLOCK), BF16), pltpu.SemaphoreType.DMA((len(BLOCK_CHUNKS),)),
-        pltpu.VMEM((E, 6 * FACEW, FACEW), BF16), pltpu.SemaphoreType.DMA((len(JAC_CHUNKS),)),
+        pltpu.VMEM((E - KEPT, BLOCK, BLOCK), BF16), pltpu.SemaphoreType.DMA((len(BLOCK_CHUNKS),)),
+        pltpu.VMEM((E, 6 * FACEW, FACEW), BF16), pltpu.SemaphoreType.DMA((2,)),
     ]
     face_scratch = [pltpu.VMEM((2 * E, 6 * FACEW), F32), pltpu.VMEM((8 * E, PEERS), F32)]
     rows_scratch = pltpu.VMEM((8 * (13 + 2 * VARS), PEERS), F32)
 
     def swap(first, second):
-        return lax.ppermute(first, "dom", even_pairs), lax.ppermute(second, "dom", odd_pairs)
+        return lax.ppermute(first, "dom", odd_pairs), lax.ppermute(second, "dom", even_pairs)
 
     small = (node, owner, elem, donor_coords, recv_counts, nbr, spread)
-    base, first, second, pay, rank = call(
+    base, first, second, pay, rank, kept = call(
         first_kernel,
         [HBM] * 10,
-        [full, half, half, table, ((1, RPTS), jnp.int32)],
+        [full, half, half, table, ((1, RPTS), jnp.int32), ((KEPT, BLOCK, BLOCK), BF16)],
         [
             pltpu.VMEM((E, BLOCK), F32), row, row, row, pltpu.VMEM((3, RPTS), F32),
             pltpu.SMEM((1, 4), jnp.int32), pltpu.VMEM((6, E), jnp.int32),
@@ -486,16 +511,16 @@
     interp, blocks = call(
         interp_kernel,
         [VM, HBM],
-        [full, ((E, BLOCK, BLOCK), BF16)],
+        [full, ((E - KEPT, BLOCK, BLOCK), BF16)],
         [rows_scratch, matrices[1]],
         got1, in_hbm(block_inv),
     )
     u, base, first, second, pay = call(
         second_kernel,
-        [VM] * 6 + [HBM] + [VM] * 3 + [SM, VM, VM],
+        [VM] * 7 + [HBM] + [VM] * 3 + [SM, VM, VM],
         [full, full, half, half, table],
         matrices[2:] + face_scratch,
-        base, first, second, interp, grad_rhs, blocks, in_hbm(jac), node, owner, rank, recv_counts, nbr, spread,
+        base, first, second, interp, grad_rhs, kept, blocks, in_hbm(jac), node, owner, rank, recv_counts, nbr, spread,
     )
     got2 = exchange(pay)
     first, second = swap(first, second)

time: 68.9 us -> 68 us (0.987)
  transfers between devices with their start and end apart: 6 -> 6, of which waited for: 2 -> 2; matrix products, arithmetic and copies ran while one was open for 0% -> 0% of each run, Pallas kernels for 6% -> 5%
where the time goes in v5:
time: 68 us; the launch traced here: 67.7 us
  starting transfers between devices  23.6 us (35%)
  Pallas kernels  16.7 us (25%)
  blocking collectives  15.8 us (23%)
  waiting for transfers between devices  11.3 us (17%)
    pallas_call x6, Pallas kernels, call(): pl.pallas_call(kernel, in_specs=in_specs, out_specs=[VM] * len(outs), out...  16.7 us
    all_to_all x2, starting transfers between devices, exchange(): lax.all_to_all(table.reshape(PEERS, 1, PEERS), AXES, split_axis=0, concat...  16.1 us
    all_to_all x1, blocking collectives, exchange(): lax.all_to_all(table.reshape(PEERS, 1, PEERS), AXES, split_axis=0, concat...  15.8 us
    all_to_all x2, waiting for transfers between devices, exchange(): lax.all_to_all(table.reshape(PEERS, 1, PEERS), AXES, split_axis=0, concat...  11.3 us
    ppermute x2, starting transfers between devices, swap(): lax.ppermute(first, 'dom', odd_pairs)  7.34 us
  transfers between devices with their start and end apart: 6, of which 2 were waited for; matrix products, arithmetic and copies ran while one was open for 0% of the time, Pallas kernels for 5%

profile of v5, /device:TPU:1, one launch (start us, length us, event | category | flops | bytes accessed | tf_op | source)
XLA Modules:
  0.0 67.7 jit_solution(4274600423209534034)
XLA Ops:
  0.0 6.7 %first_kernel.1 = (f32[32,320]{1,0:T(8,128)S(1)}, f32[32,80]{1,0:T(8,128)S(1)}, f32[32,80]{1,0:T(8,128)S(1)}, f32[128,128]{1,0:T(8,128)}, s32[1,512]{1,0:T(1,128)S(1)}, /*index=5*/bf16[8,320,320]{2,1,0:T(8,128)(2,1)S(1)}) custom-call(f32[32,320]{1,0:T(8,128)} %b_ref.5, bf16[32,320,320]{2,1,0:T(8,128)(2,1)} %blocks_hbm.3, bf16[32,480,80]{2,1,0:T(8,128)(2,1)} %bitcast.30, ...), custom_call_target="tpu_custom_call" | custom-call | tf_op jit(solution)/shard_map/first_kernel/pallas_call | solution.py:452
  6.7 0.0 copy-start
  6.7 0.0 copy-start.1
  6.7 0.0 copy-start.2
  6.7 0.0 copy-start.3
  6.7 0.0 copy-start.4
  6.7 0.0 copy-start.5
  6.8 11.5 %all-to-all-start = ((f32[128,1,128]{2,1,0:T(1,128)}), f32[128,1,128]{2,1,0:T(1,128)S(1)}, u32[]{:S(2)}, u32[]{:S(2)}) async-start(f32[128,1,128]{2,1,0:T(1,128)} %bitcast.6), calls=%async_computation | async-start | bytes 131072 | tf_op jit(solution)/shard_map/all_to_all | solution.py:464
  18.3 3.7 %collective-permute-start = (f32[32,80]{1,0:T(8,128)S(1)}, f32[32,80]{1,0:T(8,128)S(1)}, u32[]{:S(2)}, u32[]{:S(2)}) collective-permute-start(f32[32,80]{1,0:T(8,128)S(1)} %get-tuple-element.22), channel_id=1, source_target_pairs={{1,2},{2,1},{3,4},{4,3},{5,6},{6,5},{7,8},{8,7},{9,10},{10,9},{11,... | collective-permute-start | bytes 30728 | tf_op jit(solution)/shard_map/ppermute | solution.py:493
  21.9 0.1 collective-permute-start.1
  22.0 5.6 %all-to-all-done = f32[128,1,128]{2,1,0:T(1,128)S(1)} async-done(((f32[128,1,128]{2,1,0:T(1,128)}), f32[128,1,128]{2,1,0:T(1,128)S(1)}, u32[]{:S(2)}, u32[]{:S(2)}) %all-to-all-start) | async-done | bytes 65568 | tf_op jit(solution)/shard_map/all_to_all | solution.py:464
  27.7 2.7 %interp_kernel.1 = (f32[32,320]{1,0:T(8,128)S(1)}, bf16[24,320,320]{2,1,0:T(8,128)(2,1)S(1)}) custom-call(f32[128,128]{1,0:T(8,128)S(1)} %bitcast.17, bf16[32,320,320]{2,1,0:T(8,128)(2,1)} %blocks_hbm.3), custom_call_target="tpu_custom_call" | custom-call | tf_op jit(solution)/shard_map/interp_kernel/pallas_call | solution.py:452
  30.4 0.0 collective-permute-done.first_in
  30.4 0.0 collective-permute-done.1.second_in
  30.4 0.0 copy-done
  30.4 0.0 copy-done.1
  30.5 0.0 copy-done.2
  30.5 0.0 copy-done.3
  30.5 0.0 copy-done.4
  30.5 0.0 copy-done.5
  30.5 5.0 %second_kernel.1 = (f32[32,320]{1,0:T(8,128)S(1)}, f32[32,320]{1,0:T(8,128)S(1)}, f32[32,80]{1,0:T(8,128)S(1)}, f32[32,80]{1,0:T(8,128)S(1)}, f32[128,128]{1,0:T(8,128)}) custom-call(f32[32,320]{1,0:T(8,128)S(1)} %get-tuple-element.21.base_ref, f32[32,80]{1,0:T(8,128)S(1)} %collective-permute-done.first_in, f32[32,80]{1,0:T(8,128)S(1)} %collective-permute-done.1.second_in, ...), custom_call_target="tpu_custom_call" | custom-call | tf_op jit(solution)/shard_map/second_kernel/pallas_call | solution.py:452
  35.5 4.6 %all-to-all-start.1 = ((f32[128,1,128]{2,1,0:T(1,128)}), f32[128,1,128]{2,1,0:T(1,128)S(1)}, u32[]{:S(2)}, u32[]{:S(2)}) async-start(f32[128,1,128]{2,1,0:T(1,128)} %bitcast.9), calls=%async_computation.1 | async-start | bytes 131072 | tf_op jit(solution)/shard_map/all_to_all | solution.py:464
  40.1 3.7 %collective-permute-start.2 = (f32[32,80]{1,0:T(8,128)S(1)}, f32[32,80]{1,0:T(8,128)S(1)}, u32[]{:S(2)}, u32[]{:S(2)}) collective-permute-start(f32[32,80]{1,0:T(8,128)S(1)} %get-tuple-element.30), channel_id=1, source_target_pairs={{1,2},{2,1},{3,4},{4,3},{5,6},{6,5},{7,8},{8,7},{9,10},{10,9},{11,... | collective-permute-start | bytes 30728 | tf_op jit(solution)/shard_map/ppermute | solution.py:493
  43.8 0.1 collective-permute-start.3
  43.9 5.6 %all-to-all-done.1 = f32[128,1,128]{2,1,0:T(1,128)S(1)} async-done(((f32[128,1,128]{2,1,0:T(1,128)}), f32[128,1,128]{2,1,0:T(1,128)S(1)}, u32[]{:S(2)}, u32[]{:S(2)}) %all-to-all-start.1) | async-done | bytes 65568 | tf_op jit(solution)/shard_map/all_to_all | solution.py:464
  49.6 0.6 late_interp_kernel.1.interp_ref
  50.2 0.0 collective-permute-done.2.first_ref
  50.2 0.0 collective-permute-done.3.second_ref
  50.2 0.6 third_kernel.1
  50.8 15.8 %all_to_all.15 = f32[128,1,128]{2,1,0:T(1,128)S(1)} all-to-all(f32[128,1,128]{2,1,0:T(1,128)S(1)} %bitcast.22), channel_id=1, replica_groups=mesh['grp'=4,'dom'=32] {'grp','dom'}, dimensions={0} | all-to-all | bytes 131072 | tf_op jit(solution)/shard_map/all_to_all | solution.py:464
  66.6 1.1 %last_kernel.1 = f32[32,320]{1,0:T(8,128)} custom-call(f32[128,128]{1,0:T(8,128)S(1)} %bitcast.21, f32[8,128]{1,0:T(8,128)S(1)} %get-tuple-element.35.known_ref, f32[32,320]{1,0:T(8,128)S(1)} %copy-done.1, f32[32,320]{1,0:T(8,128)S(1)} %get-tuple-element.36.rest_ref), custom_call_target="tpu_custom_call" | custom-call | tf_op jit(solution)/shard_map/last_kernel/pallas_call | solution.py:452
Async XLA Ops:
  6.7 23.8 %copy-start = (bf16[480,320]{1,0:T(8,128)(2,1)S(1)}, bf16[480,320]{1,0:T(8,128)(2,1)}, u32[]{:S(2)}) copy-start(bf16[480,320]{1,0:T(8,128)(2,1)} %constant.2.clone.spread_hbm.spread_ref) | copy-start | bytes 921604
  6.7 23.8 %copy-start.1 = (f32[32,320]{1,0:T(8,128)S(1)}, f32[32,320]{1,0:T(8,128)}, u32[]{:S(2)}) copy-start(f32[32,320]{1,0:T(8,128)} %b_ref.5) | copy-start | bytes 122884
  6.7 23.8 %copy-start.2 = (s32[32,6]{0,1:T(8,128)S(1)}, s32[32,6]{0,1:T(8,128)}, u32[]{:S(2)}) copy-start(s32[32,6]{0,1:T(8,128)} %param.13) | copy-start | bytes 2308
  6.7 23.8 %copy-start.3 = (s32[512]{0:T(512)S(1)}, s32[512]{0:T(512)}, u32[]{:S(2)}) copy-start(s32[512]{0:T(512)} %param.14) | copy-start | bytes 6148
  6.7 23.7 %copy-start.4 = (s32[512,1]{0,1:T(1,128)S(1)}, s32[512,1]{0,1:T(1,128)}, u32[]{:S(2)}) copy-start(s32[512,1]{0,1:T(1,128)} %param.15) | copy-start | bytes 6148
  6.7 23.7 %copy-start.5 = (s32[1,4]{1,0:T(1,128)S(1)}, s32[1,4]{1,0:T(1,128)}, u32[]{:S(2)}) copy-start(s32[1,4]{1,0:T(1,128)} %count_ref.1) | copy-start | bytes 52
  6.8 20.9 %all-to-all-start = ((f32[128,1,128]{2,1,0:T(1,128)}), f32[128,1,128]{2,1,0:T(1,128)S(1)}, u32[]{:S(2)}, u32[]{:S(2)}) async-start(f32[128,1,128]{2,1,0:T(1,128)} %bitcast.6), calls=%async_computation | async-start | bytes 131072 | tf_op jit(solution)/shard_map/all_to_all | solution.py:464
  18.3 12.2 %collective-permute-start = (f32[32,80]{1,0:T(8,128)S(1)}, f32[32,80]{1,0:T(8,128)S(1)}, u32[]{:S(2)}, u32[]{:S(2)}) collective-permute-start(f32[32,80]{1,0:T(8,128)S(1)} %get-tuple-element.22), channel_id=1, source_target_pairs={{1,2},{2,1},{3,4},{4,3},{5,6},{6,5},{7,8},{8,7},{9,10},{10,9},{11,... | collective-permute-start | bytes 30728 | tf_op jit(solution)/shard_map/ppermute | solution.py:493
  21.9 8.5 %collective-permute-start.1 = (f32[32,80]{1,0:T(8,128)S(1)}, f32[32,80]{1,0:T(8,128)S(1)}, u32[]{:S(2)}, u32[]{:S(2)}) collective-permute-start(f32[32,80]{1,0:T(8,128)S(1)} %get-tuple-element.23), channel_id=1, source_target_pairs={{0,1},{1,0},{2,3},{3,2},{4,5},{5,4},{6,7},{7,6},{8,9},{9,8},{10,11... | collective-permute-start | bytes 30728 | tf_op jit(solution)/shard_map/ppermute | solution.py:493
  35.5 14.0 %all-to-all-start.1 = ((f32[128,1,128]{2,1,0:T(1,128)}), f32[128,1,128]{2,1,0:T(1,128)S(1)}, u32[]{:S(2)}, u32[]{:S(2)}) async-start(f32[128,1,128]{2,1,0:T(1,128)} %bitcast.9), calls=%async_computation.1 | async-start | bytes 131072 | tf_op jit(solution)/shard_map/all_to_all | solution.py:464
  40.1 10.1 %collective-permute-start.2 = (f32[32,80]{1,0:T(8,128)S(1)}, f32[32,80]{1,0:T(8,128)S(1)}, u32[]{:S(2)}, u32[]{:S(2)}) collective-permute-start(f32[32,80]{1,0:T(8,128)S(1)} %get-tuple-element.30), channel_id=1, source_target_pairs={{1,2},{2,1},{3,4},{4,3},{5,6},{6,5},{7,8},{8,7},{9,10},{10,9},{11,... | collective-permute-start | bytes 30728 | tf_op jit(solution)/shard_map/ppermute | solution.py:493
  43.8 6.4 %collective-permute-start.3 = (f32[32,80]{1,0:T(8,128)S(1)}, f32[32,80]{1,0:T(8,128)S(1)}, u32[]{:S(2)}, u32[]{:S(2)}) collective-permute-start(f32[32,80]{1,0:T(8,128)S(1)} %get-tuple-element.31), channel_id=1, source_target_pairs={{0,1},{1,0},{2,3},{3,2},{4,5},{5,4},{6,7},{7,6},{8,9},{9,8},{10,11... | collective-permute-start | bytes 30728 | tf_op jit(solution)/shard_map/ppermute | solution.py:493

commit v6 on v5

--- a/solution.py
+++ b/solution.py
@@ -266,9 +266,9 @@
 
 def first_kernel(
     x_hbm, blocks_hbm, jac_hbm, node_hbm, owner_hbm, elem_hbm, coord_hbm, count_hbm, nbr_hbm, spread_hbm,
-    base_ref, first_ref, second_ref, pay_ref, rank_ref, kept_ref,
+    base_ref, first_ref, second_ref, pay_hbm, rank_ref, kept_ref,
     x_ref, node_ref, owner_ref, elem_ref, coord_ref, count_ref, nbr_ref, spread_ref, small_sems,
-    blocks, block_sems, jac, jac_sems, traces, outs,
+    blocks, block_sems, jac, jac_sems, traces, outs, pay_ref, pay_sem,
 ):
     small = [
         pltpu.make_async_copy(src, dst, small_sems.at[i])
@@ -302,7 +302,10 @@
     comps += [coord_ref[c : c + 1, :] for c in range(3)]
     comps.append(elem_ref[...].astype(F32))
     pay_ref[...] = pack(hot16, rank, comps)
+    sent = pltpu.make_async_copy(pay_ref, pay_hbm, pay_sem)
+    sent.start()
     faces(x, z, jac, jac_copies, neighbour_one_hots(nbr_ref[...]), spread_ref, base_ref, first_ref, second_ref, traces, outs)
+    sent.wait()
 
 
 def neighbour_one_hots(nbr):
@@ -364,8 +367,8 @@
 def second_kernel(
     base_ref, first_in, second_in, interp_ref, b_ref, kept_ref, blocks_ref, jac_hbm,
     node_ref, owner_ref, rank_ref, count_ref, nbr_ref, spread_ref,
-    u_ref, out_ref, first_ref, second_ref, pay_ref,
-    jac, jac_sems, traces, outs,
+    u_ref, out_ref, first_ref, second_ref, pay_hbm,
+    jac, jac_sems, traces, outs, pay_ref, pay_sem,
 ):
     jac_copies = stream(jac_hbm, jac, jac_sems, (16, 16))
     for one in jac_copies.values():
@@ -380,8 +383,11 @@
     masks = point_masks(node_ref[...], [count_ref[0, i] for i in range(4)])
     hot = owner_one_hot(owner_ref[...]).astype(BF16)
     pay_ref[...] = with_scalars(pack(hot, rank_ref[...], pick(z, masks)), scalars)
+    sent = pltpu.make_async_copy(pay_ref, pay_hbm, pay_sem)
+    sent.start()
     jac_copies.pop(16).wait()
     faces(u, z, jac, jac_copies, neighbour_one_hots(nbr), spread_ref, out_ref, first_ref, second_ref, traces, outs)
+    sent.wait()
 
 
 def third_kernel(
@@ -448,11 +454,11 @@
     return pltpu.with_memory_space_constraint(x, pltpu.HBM)
 
 
-def call(kernel, in_specs, outs, scratch, *args):
+def call(kernel, in_specs, outs, scratch, *args, hbm_out=None):
     return pl.pallas_call(
         kernel,
         in_specs=in_specs,
-        out_specs=[VM] * len(outs),
+        out_specs=[HBM if i == hbm_out else VM for i in range(len(outs))],
         out_shape=[jax.ShapeDtypeStruct(shape, dtype) for shape, dtype in outs],
         scratch_shapes=scratch,
         compiler_params=pltpu.CompilerParams(vmem_limit_bytes=VMEM_LIMIT),
@@ -486,6 +492,7 @@
         pltpu.VMEM((E - KEPT, BLOCK, BLOCK), BF16), pltpu.SemaphoreType.DMA((len(BLOCK_CHUNKS),)),
         pltpu.VMEM((E, 6 * FACEW, FACEW), BF16), pltpu.SemaphoreType.DMA((2,)),
     ]
+    pay_scratch = [pltpu.VMEM((PEERS, PEERS), F32), pltpu.SemaphoreType.DMA]
     face_scratch = [pltpu.VMEM((2 * E, 6 * FACEW), F32), pltpu.VMEM((8 * E, PEERS), F32)]
     rows_scratch = pltpu.VMEM((8 * (13 + 2 * VARS), PEERS), F32)
 
@@ -503,8 +510,10 @@
             pltpu.VMEM((6 * FACEW, BLOCK), BF16), pltpu.SemaphoreType.DMA((8,)),
         ]
         + matrices
-        + face_scratch,
+        + face_scratch
+        + pay_scratch,
         *[in_hbm(one) for one in (grad_rhs, block_inv, jac) + small],
+        hbm_out=3,
     )
     got1 = exchange(pay)
     first, second = swap(first, second)
@@ -519,8 +528,9 @@
         second_kernel,
         [VM] * 7 + [HBM] + [VM] * 3 + [SM, VM, VM],
         [full, full, half, half, table],
-        matrices[2:] + face_scratch,
+        matrices[2:] + face_scratch + pay_scratch,
         base, first, second, interp, grad_rhs, kept, blocks, in_hbm(jac), node, owner, rank, recv_counts, nbr, spread,
+        hbm_out=4,
     )
     got2 = exchange(pay)
     first, second = swap(first, second)

time: 68 us -> 67.2 us (0.988)
  Pallas kernels: 16.7 us -> 16 us
    pallas_call x6, Pallas kernels: 16.7 us -> 16 us  [call(): pl.pallas_call(kernel, in_specs=in_specs, out_specs=[HBM if i == hbm_out...]
where the time goes in v6:
time: 67.2 us; the launch traced here: 67 us
  starting transfers between devices  23.6 us (35%)
  Pallas kernels  16 us (24%)
  blocking collectives  15.8 us (24%)
  waiting for transfers between devices  11.3 us (17%)
    all_to_all x2, starting transfers between devices, exchange(): lax.all_to_all(table.reshape(PEERS, 1, PEERS), AXES, split_axis=0, concat...  16.1 us
    pallas_call x6, Pallas kernels, call(): pl.pallas_call(kernel, in_specs=in_specs, out_specs=[HBM if i == hbm_out...  16 us
    all_to_all x1, blocking collectives, exchange(): lax.all_to_all(table.reshape(PEERS, 1, PEERS), AXES, split_axis=0, concat...  15.8 us
    all_to_all x2, waiting for transfers between devices, exchange(): lax.all_to_all(table.reshape(PEERS, 1, PEERS), AXES, split_axis=0, concat...  11.3 us
    ppermute x2, starting transfers between devices, swap(): lax.ppermute(first, 'dom', odd_pairs)  7.34 us
  transfers between devices with their start and end apart: 6, of which 2 were waited for; matrix products, arithmetic and copies ran while one was open for 0% of the time, Pallas kernels for 5%

profile of v6, /device:TPU:1, one launch (start us, length us, event | category | flops | bytes accessed | tf_op | source)
XLA Modules:
  0.0 67.0 jit_solution(7454138660412851774)
XLA Ops:
  0.0 6.4 %first_kernel.1 = (f32[32,320]{1,0:T(8,128)S(1)}, f32[32,80]{1,0:T(8,128)S(1)}, f32[32,80]{1,0:T(8,128)S(1)}, f32[128,128]{1,0:T(8,128)}, s32[1,512]{1,0:T(1,128)S(1)}, /*index=5*/bf16[8,320,320]{2,1,0:T(8,128)(2,1)S(1)}) custom-call(f32[32,320]{1,0:T(8,128)} %b_ref.5, bf16[32,320,320]{2,1,0:T(8,128)(2,1)} %blocks_hbm.3, bf16[32,480,80]{2,1,0:T(8,128)(2,1)} %bitcast.30, ...), custom_call_target="tpu_custom_call" | custom-call | tf_op jit(solution)/shard_map/first_kernel/pallas_call | solution.py:458
  6.4 0.0 copy-start
  6.4 0.0 copy-start.1
  6.4 0.0 copy-start.2
  6.5 0.0 copy-start.3
  6.5 0.0 copy-start.4
  6.5 0.0 copy-start.5
  6.5 11.5 %all-to-all-start = ((f32[128,1,128]{2,1,0:T(1,128)}), f32[128,1,128]{2,1,0:T(1,128)S(1)}, u32[]{:S(2)}, u32[]{:S(2)}) async-start(f32[128,1,128]{2,1,0:T(1,128)} %bitcast.6), calls=%async_computation | async-start | bytes 131072 | tf_op jit(solution)/shard_map/all_to_all | solution.py:470
  18.0 3.7 %collective-permute-start = (f32[32,80]{1,0:T(8,128)S(1)}, f32[32,80]{1,0:T(8,128)S(1)}, u32[]{:S(2)}, u32[]{:S(2)}) collective-permute-start(f32[32,80]{1,0:T(8,128)S(1)} %get-tuple-element.22), channel_id=1, source_target_pairs={{1,2},{2,1},{3,4},{4,3},{5,6},{6,5},{7,8},{8,7},{9,10},{10,9},{11,... | collective-permute-start | bytes 30728 | tf_op jit(solution)/shard_map/ppermute | solution.py:500
  21.7 0.1 collective-permute-start.1
  21.8 5.6 %all-to-all-done = f32[128,1,128]{2,1,0:T(1,128)S(1)} async-done(((f32[128,1,128]{2,1,0:T(1,128)}), f32[128,1,128]{2,1,0:T(1,128)S(1)}, u32[]{:S(2)}, u32[]{:S(2)}) %all-to-all-start) | async-done | bytes 65568 | tf_op jit(solution)/shard_map/all_to_all | solution.py:470
  27.4 2.7 %interp_kernel.1 = (f32[32,320]{1,0:T(8,128)S(1)}, bf16[24,320,320]{2,1,0:T(8,128)(2,1)S(1)}) custom-call(f32[128,128]{1,0:T(8,128)S(1)} %bitcast.17, bf16[32,320,320]{2,1,0:T(8,128)(2,1)} %blocks_hbm.3), custom_call_target="tpu_custom_call" | custom-call | tf_op jit(solution)/shard_map/interp_kernel/pallas_call | solution.py:458
  30.2 0.0 collective-permute-done.first_in
  30.2 0.0 collective-permute-done.1.second_in
  30.2 0.0 copy-done
  30.2 0.0 copy-done.1
  30.2 0.0 copy-done.2
  30.2 0.0 copy-done.3
  30.2 0.0 copy-done.4
  30.2 0.0 copy-done.5
  30.2 4.6 %second_kernel.1 = (f32[32,320]{1,0:T(8,128)S(1)}, f32[32,320]{1,0:T(8,128)S(1)}, f32[32,80]{1,0:T(8,128)S(1)}, f32[32,80]{1,0:T(8,128)S(1)}, f32[128,128]{1,0:T(8,128)}) custom-call(f32[32,320]{1,0:T(8,128)S(1)} %get-tuple-element.21.base_ref, f32[32,80]{1,0:T(8,128)S(1)} %collective-permute-done.first_in, f32[32,80]{1,0:T(8,128)S(1)} %collective-permute-done.1.second_in, ...), custom_call_target="tpu_custom_call" | custom-call | tf_op jit(solution)/shard_map/second_kernel/pallas_call | solution.py:458
  34.8 4.6 %all-to-all-start.1 = ((f32[128,1,128]{2,1,0:T(1,128)}), f32[128,1,128]{2,1,0:T(1,128)S(1)}, u32[]{:S(2)}, u32[]{:S(2)}) async-start(f32[128,1,128]{2,1,0:T(1,128)} %bitcast.9), calls=%async_computation.1 | async-start | bytes 131072 | tf_op jit(solution)/shard_map/all_to_all | solution.py:470
  39.4 3.7 %collective-permute-start.2 = (f32[32,80]{1,0:T(8,128)S(1)}, f32[32,80]{1,0:T(8,128)S(1)}, u32[]{:S(2)}, u32[]{:S(2)}) collective-permute-start(f32[32,80]{1,0:T(8,128)S(1)} %get-tuple-element.30), channel_id=1, source_target_pairs={{1,2},{2,1},{3,4},{4,3},{5,6},{6,5},{7,8},{8,7},{9,10},{10,9},{11,... | collective-permute-start | bytes 30728 | tf_op jit(solution)/shard_map/ppermute | solution.py:500
  43.1 0.1 collective-permute-start.3
  43.2 5.6 %all-to-all-done.1 = f32[128,1,128]{2,1,0:T(1,128)S(1)} async-done(((f32[128,1,128]{2,1,0:T(1,128)}), f32[128,1,128]{2,1,0:T(1,128)S(1)}, u32[]{:S(2)}, u32[]{:S(2)}) %all-to-all-start.1) | async-done | bytes 65568 | tf_op jit(solution)/shard_map/all_to_all | solution.py:470
  48.8 0.6 late_interp_kernel.1.interp_ref
  49.5 0.0 collective-permute-done.2.first_ref
  49.5 0.0 collective-permute-done.3.second_ref
  49.5 0.6 third_kernel.1
  50.1 15.8 %all_to_all.15 = f32[128,1,128]{2,1,0:T(1,128)S(1)} all-to-all(f32[128,1,128]{2,1,0:T(1,128)S(1)} %bitcast.22), channel_id=1, replica_groups=mesh['grp'=4,'dom'=32] {'grp','dom'}, dimensions={0} | all-to-all | bytes 131072 | tf_op jit(solution)/shard_map/all_to_all | solution.py:470
  65.9 1.1 %last_kernel.1 = f32[32,320]{1,0:T(8,128)} custom-call(f32[128,128]{1,0:T(8,128)S(1)} %bitcast.21, f32[8,128]{1,0:T(8,128)S(1)} %get-tuple-element.35.known_ref, f32[32,320]{1,0:T(8,128)S(1)} %copy-done.1, f32[32,320]{1,0:T(8,128)S(1)} %get-tuple-element.36.rest_ref), custom_call_target="tpu_custom_call" | custom-call | tf_op jit(solution)/shard_map/last_kernel/pallas_call | solution.py:458
Async XLA Ops:
  6.4 23.8 %copy-start = (bf16[480,320]{1,0:T(8,128)(2,1)S(1)}, bf16[480,320]{1,0:T(8,128)(2,1)}, u32[]{:S(2)}) copy-start(bf16[480,320]{1,0:T(8,128)(2,1)} %constant.2.clone.spread_hbm.spread_ref) | copy-start | bytes 921604
  6.4 23.8 %copy-start.1 = (f32[32,320]{1,0:T(8,128)S(1)}, f32[32,320]{1,0:T(8,128)}, u32[]{:S(2)}) copy-start(f32[32,320]{1,0:T(8,128)} %b_ref.5) | copy-start | bytes 122884
  6.4 23.8 %copy-start.2 = (s32[32,6]{0,1:T(8,128)S(1)}, s32[32,6]{0,1:T(8,128)}, u32[]{:S(2)}) copy-start(s32[32,6]{0,1:T(8,128)} %param.13) | copy-start | bytes 2308
  6.5 23.8 %copy-start.3 = (s32[512]{0:T(512)S(1)}, s32[512]{0:T(512)}, u32[]{:S(2)}) copy-start(s32[512]{0:T(512)} %param.14) | copy-start | bytes 6148
  6.5 23.7 %copy-start.4 = (s32[512,1]{0,1:T(1,128)S(1)}, s32[512,1]{0,1:T(1,128)}, u32[]{:S(2)}) copy-start(s32[512,1]{0,1:T(1,128)} %param.15) | copy-start | bytes 6148
  6.5 23.7 %copy-start.5 = (s32[1,4]{1,0:T(1,128)S(1)}, s32[1,4]{1,0:T(1,128)}, u32[]{:S(2)}) copy-start(s32[1,4]{1,0:T(1,128)} %count_ref.1) | copy-start | bytes 52
  6.5 20.9 %all-to-all-start = ((f32[128,1,128]{2,1,0:T(1,128)}), f32[128,1,128]{2,1,0:T(1,128)S(1)}, u32[]{:S(2)}, u32[]{:S(2)}) async-start(f32[128,1,128]{2,1,0:T(1,128)} %bitcast.6), calls=%async_computation | async-start | bytes 131072 | tf_op jit(solution)/shard_map/all_to_all | solution.py:470
  18.0 12.2 %collective-permute-start = (f32[32,80]{1,0:T(8,128)S(1)}, f32[32,80]{1,0:T(8,128)S(1)}, u32[]{:S(2)}, u32[]{:S(2)}) collective-permute-start(f32[32,80]{1,0:T(8,128)S(1)} %get-tuple-element.22), channel_id=1, source_target_pairs={{1,2},{2,1},{3,4},{4,3},{5,6},{6,5},{7,8},{8,7},{9,10},{10,9},{11,... | collective-permute-start | bytes 30728 | tf_op jit(solution)/shard_map/ppermute | solution.py:500
  21.7 8.5 %collective-permute-start.1 = (f32[32,80]{1,0:T(8,128)S(1)}, f32[32,80]{1,0:T(8,128)S(1)}, u32[]{:S(2)}, u32[]{:S(2)}) collective-permute-start(f32[32,80]{1,0:T(8,128)S(1)} %get-tuple-element.23), channel_id=1, source_target_pairs={{0,1},{1,0},{2,3},{3,2},{4,5},{5,4},{6,7},{7,6},{8,9},{9,8},{10,11... | collective-permute-start | bytes 30728 | tf_op jit(solution)/shard_map/ppermute | solution.py:500
  34.8 14.0 %all-to-all-start.1 = ((f32[128,1,128]{2,1,0:T(1,128)}), f32[128,1,128]{2,1,0:T(1,128)S(1)}, u32[]{:S(2)}, u32[]{:S(2)}) async-start(f32[128,1,128]{2,1,0:T(1,128)} %bitcast.9), calls=%async_computation.1 | async-start | bytes 131072 | tf_op jit(solution)/shard_map/all_to_all | solution.py:470
  39.4 10.1 %collective-permute-start.2 = (f32[32,80]{1,0:T(8,128)S(1)}, f32[32,80]{1,0:T(8,128)S(1)}, u32[]{:S(2)}, u32[]{:S(2)}) collective-permute-start(f32[32,80]{1,0:T(8,128)S(1)} %get-tuple-element.30), channel_id=1, source_target_pairs={{1,2},{2,1},{3,4},{4,3},{5,6},{6,5},{7,8},{8,7},{9,10},{10,9},{11,... | collective-permute-start | bytes 30728 | tf_op jit(solution)/shard_map/ppermute | solution.py:500
  43.1 6.4 %collective-permute-start.3 = (f32[32,80]{1,0:T(8,128)S(1)}, f32[32,80]{1,0:T(8,128)S(1)}, u32[]{:S(2)}, u32[]{:S(2)}) collective-permute-start(f32[32,80]{1,0:T(8,128)S(1)} %get-tuple-element.31), channel_id=1, source_target_pairs={{0,1},{1,0},{2,3},{3,2},{4,5},{5,4},{6,7},{7,6},{8,9},{9,8},{10,11... | collective-permute-start | bytes 30728 | tf_op jit(solution)/shard_map/ppermute | solution.py:500

commit v7 on v6

--- a/solution.py
+++ b/solution.py
@@ -15,9 +15,9 @@
 PEERS = 128
 CAP = 8
 RPTS = 512
-BLOCK_CHUNKS = (8, 8, 16)
+BLOCK_CHUNKS = (8, 16, 8)
 KEPT = 8
-START_JAC = 0
+START_JAC = 8
 AHEAD = 3
 JAC_CHUNKS = (16, 16)
 SCALAR_LANE = 96

time: 67.2 us -> 67.2 us (level)
  no operation moved by 1% of the time
where the time goes in v7:
time: 67.2 us; the launch traced here: 67 us
  starting transfers between devices  23.6 us (35%)
  Pallas kernels  16 us (24%)
  blocking collectives  15.8 us (24%)
  waiting for transfers between devices  11.3 us (17%)
    all_to_all x2, starting transfers between devices, exchange(): lax.all_to_all(table.reshape(PEERS, 1, PEERS), AXES, split_axis=0, concat...  16.1 us
    pallas_call x6, Pallas kernels, call(): pl.pallas_call(kernel, in_specs=in_specs, out_specs=[HBM if i == hbm_out...  16 us
    all_to_all x1, blocking collectives, exchange(): lax.all_to_all(table.reshape(PEERS, 1, PEERS), AXES, split_axis=0, concat...  15.8 us
    all_to_all x2, waiting for transfers between devices, exchange(): lax.all_to_all(table.reshape(PEERS, 1, PEERS), AXES, split_axis=0, concat...  11.3 us
    ppermute x2, starting transfers between devices, swap(): lax.ppermute(first, 'dom', odd_pairs)  7.34 us
  transfers between devices with their start and end apart: 6, of which 2 were waited for; matrix products, arithmetic and copies ran while one was open for 0% of the time, Pallas kernels for 5%

profile of v7, /device:TPU:1, one launch (start us, length us, event | category | flops | bytes accessed | tf_op | source)
XLA Modules:
  0.0 67.0 jit_solution(3084537066995617715)
XLA Ops:
  0.0 6.4 %first_kernel.1 = (f32[32,320]{1,0:T(8,128)S(1)}, f32[32,80]{1,0:T(8,128)S(1)}, f32[32,80]{1,0:T(8,128)S(1)}, f32[128,128]{1,0:T(8,128)}, s32[1,512]{1,0:T(1,128)S(1)}, /*index=5*/bf16[8,320,320]{2,1,0:T(8,128)(2,1)S(1)}) custom-call(f32[32,320]{1,0:T(8,128)} %b_ref.5, bf16[32,320,320]{2,1,0:T(8,128)(2,1)} %blocks_hbm.3, bf16[32,480,80]{2,1,0:T(8,128)(2,1)} %bitcast.30, ...), custom_call_target="tpu_custom_call" | custom-call | tf_op jit(solution)/shard_map/first_kernel/pallas_call | solution.py:458
  6.4 0.0 copy-start
  6.4 0.0 copy-start.1
  6.4 0.0 copy-start.2
  6.4 0.0 copy-start.3
  6.4 0.0 copy-start.4
  6.4 0.0 copy-start.5
  6.4 11.5 %all-to-all-start = ((f32[128,1,128]{2,1,0:T(1,128)}), f32[128,1,128]{2,1,0:T(1,128)S(1)}, u32[]{:S(2)}, u32[]{:S(2)}) async-start(f32[128,1,128]{2,1,0:T(1,128)} %bitcast.6), calls=%async_computation | async-start | bytes 131072 | tf_op jit(solution)/shard_map/all_to_all | solution.py:470
  18.0 3.7 %collective-permute-start = (f32[32,80]{1,0:T(8,128)S(1)}, f32[32,80]{1,0:T(8,128)S(1)}, u32[]{:S(2)}, u32[]{:S(2)}) collective-permute-start(f32[32,80]{1,0:T(8,128)S(1)} %get-tuple-element.22), channel_id=1, source_target_pairs={{1,2},{2,1},{3,4},{4,3},{5,6},{6,5},{7,8},{8,7},{9,10},{10,9},{11,... | collective-permute-start | bytes 30728 | tf_op jit(solution)/shard_map/ppermute | solution.py:500
  21.6 0.1 collective-permute-start.1
  21.7 5.6 %all-to-all-done = f32[128,1,128]{2,1,0:T(1,128)S(1)} async-done(((f32[128,1,128]{2,1,0:T(1,128)}), f32[128,1,128]{2,1,0:T(1,128)S(1)}, u32[]{:S(2)}, u32[]{:S(2)}) %all-to-all-start) | async-done | bytes 65568 | tf_op jit(solution)/shard_map/all_to_all | solution.py:470
  27.4 2.8 %interp_kernel.1 = (f32[32,320]{1,0:T(8,128)S(1)}, bf16[24,320,320]{2,1,0:T(8,128)(2,1)S(1)}) custom-call(f32[128,128]{1,0:T(8,128)S(1)} %bitcast.17, bf16[32,320,320]{2,1,0:T(8,128)(2,1)} %blocks_hbm.3), custom_call_target="tpu_custom_call" | custom-call | tf_op jit(solution)/shard_map/interp_kernel/pallas_call | solution.py:458
  30.1 0.0 collective-permute-done.first_in
  30.1 0.0 collective-permute-done.1.second_in
  30.2 0.0 copy-done
  30.2 0.0 copy-done.1
  30.2 0.0 copy-done.2
  30.2 0.0 copy-done.3
  30.2 0.0 copy-done.4
  30.2 0.0 copy-done.5
  30.2 4.6 %second_kernel.1 = (f32[32,320]{1,0:T(8,128)S(1)}, f32[32,320]{1,0:T(8,128)S(1)}, f32[32,80]{1,0:T(8,128)S(1)}, f32[32,80]{1,0:T(8,128)S(1)}, f32[128,128]{1,0:T(8,128)}) custom-call(f32[32,320]{1,0:T(8,128)S(1)} %get-tuple-element.21.base_ref, f32[32,80]{1,0:T(8,128)S(1)} %collective-permute-done.first_in, f32[32,80]{1,0:T(8,128)S(1)} %collective-permute-done.1.second_in, ...), custom_call_target="tpu_custom_call" | custom-call | tf_op jit(solution)/shard_map/second_kernel/pallas_call | solution.py:458
  34.8 4.6 %all-to-all-start.1 = ((f32[128,1,128]{2,1,0:T(1,128)}), f32[128,1,128]{2,1,0:T(1,128)S(1)}, u32[]{:S(2)}, u32[]{:S(2)}) async-start(f32[128,1,128]{2,1,0:T(1,128)} %bitcast.9), calls=%async_computation.1 | async-start | bytes 131072 | tf_op jit(solution)/shard_map/all_to_all | solution.py:470
  39.4 3.7 %collective-permute-start.2 = (f32[32,80]{1,0:T(8,128)S(1)}, f32[32,80]{1,0:T(8,128)S(1)}, u32[]{:S(2)}, u32[]{:S(2)}) collective-permute-start(f32[32,80]{1,0:T(8,128)S(1)} %get-tuple-element.30), channel_id=1, source_target_pairs={{1,2},{2,1},{3,4},{4,3},{5,6},{6,5},{7,8},{8,7},{9,10},{10,9},{11,... | collective-permute-start | bytes 30728 | tf_op jit(solution)/shard_map/ppermute | solution.py:500
  43.1 0.1 collective-permute-start.3
  43.2 5.6 %all-to-all-done.1 = f32[128,1,128]{2,1,0:T(1,128)S(1)} async-done(((f32[128,1,128]{2,1,0:T(1,128)}), f32[128,1,128]{2,1,0:T(1,128)S(1)}, u32[]{:S(2)}, u32[]{:S(2)}) %all-to-all-start.1) | async-done | bytes 65568 | tf_op jit(solution)/shard_map/all_to_all | solution.py:470
  48.8 0.6 late_interp_kernel.1.interp_ref
  49.5 0.0 collective-permute-done.2.first_ref
  49.5 0.0 collective-permute-done.3.second_ref
  49.5 0.6 third_kernel.1
  50.1 15.8 %all_to_all.15 = f32[128,1,128]{2,1,0:T(1,128)S(1)} all-to-all(f32[128,1,128]{2,1,0:T(1,128)S(1)} %bitcast.22), channel_id=1, replica_groups=mesh['grp'=4,'dom'=32] {'grp','dom'}, dimensions={0} | all-to-all | bytes 131072 | tf_op jit(solution)/shard_map/all_to_all | solution.py:470
  65.9 1.1 %last_kernel.1 = f32[32,320]{1,0:T(8,128)} custom-call(f32[128,128]{1,0:T(8,128)S(1)} %bitcast.21, f32[8,128]{1,0:T(8,128)S(1)} %get-tuple-element.35.known_ref, f32[32,320]{1,0:T(8,128)S(1)} %copy-done.1, f32[32,320]{1,0:T(8,128)S(1)} %get-tuple-element.36.rest_ref), custom_call_target="tpu_custom_call" | custom-call | tf_op jit(solution)/shard_map/last_kernel/pallas_call | solution.py:458
Async XLA Ops:
  6.4 23.8 %copy-start = (bf16[480,320]{1,0:T(8,128)(2,1)S(1)}, bf16[480,320]{1,0:T(8,128)(2,1)}, u32[]{:S(2)}) copy-start(bf16[480,320]{1,0:T(8,128)(2,1)} %constant.2.clone.spread_hbm.spread_ref) | copy-start | bytes 921604
  6.4 23.8 %copy-start.1 = (f32[32,320]{1,0:T(8,128)S(1)}, f32[32,320]{1,0:T(8,128)}, u32[]{:S(2)}) copy-start(f32[32,320]{1,0:T(8,128)} %b_ref.5) | copy-start | bytes 122884
  6.4 23.8 %copy-start.2 = (s32[32,6]{0,1:T(8,128)S(1)}, s32[32,6]{0,1:T(8,128)}, u32[]{:S(2)}) copy-start(s32[32,6]{0,1:T(8,128)} %param.13) | copy-start | bytes 2308
  6.4 23.8 %copy-start.3 = (s32[512]{0:T(512)S(1)}, s32[512]{0:T(512)}, u32[]{:S(2)}) copy-start(s32[512]{0:T(512)} %param.14) | copy-start | bytes 6148
  6.4 23.8 %copy-start.4 = (s32[512,1]{0,1:T(1,128)S(1)}, s32[512,1]{0,1:T(1,128)}, u32[]{:S(2)}) copy-start(s32[512,1]{0,1:T(1,128)} %param.15) | copy-start | bytes 6148
  6.4 23.8 %copy-start.5 = (s32[1,4]{1,0:T(1,128)S(1)}, s32[1,4]{1,0:T(1,128)}, u32[]{:S(2)}) copy-start(s32[1,4]{1,0:T(1,128)} %count_ref.1) | copy-start | bytes 52
  6.4 20.9 %all-to-all-start = ((f32[128,1,128]{2,1,0:T(1,128)}), f32[128,1,128]{2,1,0:T(1,128)S(1)}, u32[]{:S(2)}, u32[]{:S(2)}) async-start(f32[128,1,128]{2,1,0:T(1,128)} %bitcast.6), calls=%async_computation | async-start | bytes 131072 | tf_op jit(solution)/shard_map/all_to_all | solution.py:470
  18.0 12.2 %collective-permute-start = (f32[32,80]{1,0:T(8,128)S(1)}, f32[32,80]{1,0:T(8,128)S(1)}, u32[]{:S(2)}, u32[]{:S(2)}) collective-permute-start(f32[32,80]{1,0:T(8,128)S(1)} %get-tuple-element.22), channel_id=1, source_target_pairs={{1,2},{2,1},{3,4},{4,3},{5,6},{6,5},{7,8},{8,7},{9,10},{10,9},{11,... | collective-permute-start | bytes 30728 | tf_op jit(solution)/shard_map/ppermute | solution.py:500
  21.6 8.5 %collective-permute-start.1 = (f32[32,80]{1,0:T(8,128)S(1)}, f32[32,80]{1,0:T(8,128)S(1)}, u32[]{:S(2)}, u32[]{:S(2)}) collective-permute-start(f32[32,80]{1,0:T(8,128)S(1)} %get-tuple-element.23), channel_id=1, source_target_pairs={{0,1},{1,0},{2,3},{3,2},{4,5},{5,4},{6,7},{7,6},{8,9},{9,8},{10,11... | collective-permute-start | bytes 30728 | tf_op jit(solution)/shard_map/ppermute | solution.py:500
  34.8 14.0 %all-to-all-start.1 = ((f32[128,1,128]{2,1,0:T(1,128)}), f32[128,1,128]{2,1,0:T(1,128)S(1)}, u32[]{:S(2)}, u32[]{:S(2)}) async-start(f32[128,1,128]{2,1,0:T(1,128)} %bitcast.9), calls=%async_computation.1 | async-start | bytes 131072 | tf_op jit(solution)/shard_map/all_to_all | solution.py:470
  39.4 10.1 %collective-permute-start.2 = (f32[32,80]{1,0:T(8,128)S(1)}, f32[32,80]{1,0:T(8,128)S(1)}, u32[]{:S(2)}, u32[]{:S(2)}) collective-permute-start(f32[32,80]{1,0:T(8,128)S(1)} %get-tuple-element.30), channel_id=1, source_target_pairs={{1,2},{2,1},{3,4},{4,3},{5,6},{6,5},{7,8},{8,7},{9,10},{10,9},{11,... | collective-permute-start | bytes 30728 | tf_op jit(solution)/shard_map/ppermute | solution.py:500
  43.1 6.4 %collective-permute-start.3 = (f32[32,80]{1,0:T(8,128)S(1)}, f32[32,80]{1,0:T(8,128)S(1)}, u32[]{:S(2)}, u32[]{:S(2)}) collective-permute-start(f32[32,80]{1,0:T(8,128)S(1)} %get-tuple-element.31), channel_id=1, source_target_pairs={{0,1},{1,0},{2,3},{3,2},{4,5},{5,4},{6,7},{7,6},{8,9},{9,8},{10,11... | collective-permute-start | bytes 30728 | tf_op jit(solution)/shard_map/ppermute | solution.py:500
